TPU v7x, 32 devices: a whole 2x2x4 slice. The times are simulated.
32 devices in a mesh: tm: 4 (over x, core), inp: 8 (over z, y).
Axes of the slice: x: 2, y: 2, z: 4, core: 2. Of those that a mesh axis runs over, the one named last changes fastest.
Arguments:
- voltage: int32 [256, 524288], P('inp', 'tm'), may hold values from -127 to 127
- taps: float32 [4, 512], replicated, may hold values from -0.0625 to 0.0625
- chan_table: int32 [256], replicated, may hold values from 0 to 255, each once
Outputs:
- visibility: float32 [256, 128, 256], P('tm', 'inp')
- beam: float32 [128, 1024], P('inp', 'tm')
Inputs may be any that keep to these rules, and one draw needn't show every extreme that they name: `chan_table`: each channel number appears once.
All inputs are finite; a program needn't handle non-finite values.
Results may differ from a plain program's by a relative error of at most 0.0016.
Values may be sent and summed in bfloat16 or wider, within the bound.
No kernel may reach another device: no remote copies, remote signals or barrier semaphores. Data moves between devices by JAX's collectives and lax.ppermute only.
A program may use at most 64 MiB of HBM per device.

v0:
```python
import math

import jax
import jax.numpy as jnp
from jax import lax
from jax.sharding import PartitionSpec as P

NIN = 256
P_SIZE = 512
TAPS = 4
NCH = 128


def passed_along(block, axis, distance):
    devices = range(lax.axis_size(axis))
    route = [(i - distance, i) for i in devices if i - distance in devices]
    return lax.ppermute(block, axis, route)


def dft_table(chan_table):
    chosen = chan_table[:NCH]
    points = jnp.arange(P_SIZE, dtype=jnp.int32)
    phase = chosen[:, None] * points[None, :] % P_SIZE
    angle = phase.astype(jnp.float32) * (2.0 * math.pi / P_SIZE)
    factor = 1.0 / math.sqrt(P_SIZE)
    table = jnp.stack([jnp.cos(angle) * factor, -jnp.sin(angle) * factor], axis=1)
    return table.astype(jnp.bfloat16)


def split_parts(received):
    parts = received[0]
    combined = jnp.concatenate([parts[:, 0], parts[:, 1]], axis=-1)
    rotated = jnp.concatenate([parts[:, 1], -parts[:, 0]], axis=-1)
    return (combined, rotated)


def packed_rows(combined, rotated, count):
    real_part = jnp.einsum("cas,cbs->acb", combined, combined, preferred_element_type=jnp.float32)
    imag_part = jnp.einsum("cas,cbs->acb", rotated, combined, preferred_element_type=jnp.float32)
    row_index = jnp.arange(count, dtype=jnp.int32)
    col_index = jnp.arange(combined.shape[1], dtype=jnp.int32)
    upper = (row_index[:, None] <= col_index[None, :])[:, None, :]
    return jnp.where(upper, real_part, imag_part)


def on_device(voltage, taps, chan_table):
    inputs_here = voltage.shape[0]
    spectra_here = voltage.shape[1] // P_SIZE
    groups = lax.axis_size("inp")
    volts = voltage.astype(jnp.bfloat16)
    tail = volts[:, (spectra_here - TAPS + 1) * P_SIZE :]
    earlier = passed_along(tail, "tm", 1)
    extended = jnp.concatenate([earlier, volts], axis=1).reshape(
        inputs_here, spectra_here + TAPS - 1, P_SIZE
    )
    filtered = jnp.zeros((inputs_here, spectra_here, P_SIZE), jnp.float32)
    for tap_index in range(TAPS):
        filtered = filtered + taps[tap_index] * extended[
            :, tap_index : tap_index + spectra_here, :
        ].astype(jnp.float32)
    filtered = filtered.astype(jnp.bfloat16)
    table = dft_table(chan_table).reshape(groups, NCH // groups, 2, P_SIZE)
    spectra = jnp.einsum(
        "gcqp,isp->gcqis", table, filtered, preferred_element_type=jnp.float32
    ).astype(jnp.bfloat16)
    total = spectra_here * lax.axis_size("tm")
    power = jnp.sum(jnp.square(spectra.astype(jnp.float32)), axis=(2, 3)).reshape(NCH, spectra_here)
    beam = lax.psum_scatter(power, "inp", scatter_dimension=0, tiled=True) / NIN
    received = lax.all_to_all(spectra, "inp", split_axis=0, concat_axis=3, tiled=True)
    combined, rotated = split_parts(received)
    packed = packed_rows(combined, rotated, combined.shape[1])
    visibility = lax.psum_scatter(packed, "tm", scatter_dimension=0, tiled=True)
    return (visibility / total, beam)


def solution(mesh):
    in_specs = (P("inp", "tm"), P(), P())
    out_specs = (P("tm", "inp", None), P("inp", "tm"))
    return jax.shard_map(
        on_device, mesh=mesh, in_specs=in_specs, out_specs=out_specs, check_vma=False
    )
```

profile of v0, /device:TPU:0, one launch (start us, length us, event | category | flops | bytes accessed | tf_op | source)
XLA Modules:
  0.0 236.0 jit_solution(5710754618316786529)
XLA Ops:
  7.2 0.0 slice-start
  7.2 0.0 copy-start.1
  7.2 6.3 %convert_element_type.43 = bf16[32,131072]{1,0:T(8,128)(2,1)S(1)} convert(s32[32,131072]{1,0:T(8,128)} %param.3) | non-fusion elementwise | flops 4194304 | bytes 25165824 | tf_op jit(solution)/shard_map/convert_element_type | solution.py:50
  13.5 0.0 copy-start
  13.5 3.2 %copy-done = bf16[32,131072]{1,0:T(8,128)(2,1)} copy-done((bf16[32,131072]{1,0:T(8,128)(2,1)}, bf16[32,131072]{1,0:T(8,128)(2,1)S(1)}, u32[]{:S(2)}) %copy-start) | copy-done | bytes 8388632
  16.8 2.4 collective-permute-start
  19.1 0.0 slice-done
  19.1 0.1 mul.109
  19.2 1.2 multiply_convert_fusion.1
  20.5 0.0 copy-done.1
  20.5 0.0 collective-permute-done
  20.5 7.2 %pad_maximum_fusion = bf16[32,132608]{1,0:T(8,128)(2,1)} fusion(bf16[32,131072]{1,0:T(8,128)(2,1)} %copy-done, bf16[32,1536]{1,0:T(8,128)(2,1)S(1)} %collective-permute-done), kind=kLoop, calls=%fused_computation.1 | loop fusion | flops 16973824 | bytes 16973824 | tf_op jit(solution)/shard_map/concatenate | solution.py:53
  27.7 9.1 %reshape.125 = bf16[32,259,512]{2,1,0:T(8,128)(2,1)} reshape(bf16[32,132608]{1,0:T(8,128)(2,1)} %pad_maximum_fusion) | data formatting | bytes 16973824 | tf_op jit(solution)/shard_map/reshape | solution.py:53
  36.8 24.7 %multiply_reduce_fusion = (f32[8,16,256]{2,1,0:T(8,128)}, bf16[8,16,2,32,256]{4,1,3,2,0:T(8,128)(2,1)}) fusion(bf16[32,259,512]{2,1,0:T(8,128)(2,1)} %reshape.125, f32[512]{0:T(512)S(1)} %bitcast.44, f32[512]{0:T(512)S(1)} %bitcast.45, f32[512]{0:T(512)S(1)} %bitcast.43, f32[512]{0:T(512)S(1)} %bitcast.42, ...), kind=kOutput, calls=%fused_computation.3 | convolution fusion | flops 2206695424 | bytes 38150144 | tf_op jit(solution)/shard_map/gcqp,isp->gcqis/dot_general | solution.py:63
  61.5 6.7 %all-to-all-start = ((bf16[8,16,2,32,256]{4,1,3,2,0:T(8,128)(2,1)}), bf16[8,16,2,32,256]{4,1,3,2,0:T(8,128)(2,1)}, u32[]{:S(2)}, u32[]{:S(2)}) async-start(bf16[8,16,2,32,256]{4,1,3,2,0:T(8,128)(2,1)} %get-tuple-element.15), calls=%async_computation | async-start | bytes 8388608 | tf_op jit(solution)/shard_map/all_to_all | solution.py:69
  68.1 0.0 reduce-scatter.5.cloned.1.call-start
  68.2 0.6 reduce-scatter.5.cloned.1.call-update
  68.8 0.0 reduce-scatter.3.cloned.1.call-start
  68.9 94.7 %all-to-all-done = bf16[8,16,2,32,256]{4,1,3,2,0:T(8,128)(2,1)} async-done(((bf16[8,16,2,32,256]{4,1,3,2,0:T(8,128)(2,1)}), bf16[8,16,2,32,256]{4,1,3,2,0:T(8,128)(2,1)}, u32[]{:S(2)}, u32[]{:S(2)}) %all-to-all-start) | async-done | bytes 4194336 | tf_op jit(solution)/shard_map/all_to_all | solution.py:69
  163.6 3.7 %copy.10 = bf16[1,16,2,8,32,256]{5,4,3,2,1,0:T(8,128)(2,1)S(1)} copy(bf16[1,16,2,8,32,256]{5,1,4,2,3,0:T(8,128)(2,1)} %bitcast.9) | data formatting | bytes 8388608 | tf_op jit(solution)/shard_map/all_to_all | solution.py:69
  167.3 0.1 fusion.22
  167.4 0.3 slice_bitcast_fusion.1
  167.7 1.9 fusion.3
  169.6 2.9 %bitcast_select_fusion = f32[256,16,256]{0,2,1:T(8,128)} fusion(f32[16,256,256]{2,1,0:T(8,128)S(1)} %fusion.3, pred[256,256]{0,1:T(8,128)(4,1)S(1)} %iota_compare_fusion, bf16[16,256,256]{2,1,0:T(8,128)(2,1)S(1)} %get-tuple-element.7, bf16[16,256,256]{2,1,0:T(8,128)(2,1)S(1)} %get-tuple-element.6), kind=kOutput, calls=%fused_computation.10 | convolution fusion | flops 1083179008 | bytes 12648448 | tf_op jit(solution)/shard_map/cas,cbs->acb/dot_general | solution.py:38
  172.6 5.5 %copy.13 = f32[256,16,256]{2,1,0:T(8,128)} copy(f32[256,16,256]{0,2,1:T(8,128)} %bitcast_select_fusion) | data formatting | bytes 8388608 | tf_op jit(solution)/shard_map/jit(_where)/select_n | solution.py:43
  178.1 0.0 reduce-scatter.3.cloned.1.call-update
  178.1 2.7 %reduce-scatter.5.cloned.1.call-done = f32[16,256]{1,0:T(8,128)} async-done(((f32[128,256]{1,0:T(8,128)}), f32[16,256]{1,0:T(8,128)}) %reduce-scatter.5.cloned.1.call-update) | async-done | bytes 16400 | tf_op jit(solution)/shard_map/reduce_scatter | solution.py:68
  180.8 1.3 broadcast_multiply_fusion.1
  182.1 44.8 %reduce-scatter.3.cloned.1.call-done = f32[64,16,256]{2,1,0:T(8,128)} async-done(((f32[256,16,256]{2,1,0:T(8,128)}), f32[64,16,256]{2,1,0:T(8,128)}) %reduce-scatter.3.cloned.1.call-update) | async-done | bytes 1048592 | tf_op jit(solution)/shard_map/reduce_scatter | solution.py:72
  226.9 2.3 broadcast_multiply_fusion
  (3 shorter events, 0.0 us)
Async XLA Ops:
  7.2 12.0 %slice-start = ((s32[256]{0:T(256)}), s32[128]{0:T(128)S(1)}, s32[]{:S(2)}) async-start(s32[256]{0:T(256)} %param.5), calls=%async_computation.5 | async-start | bytes 1024 | tf_op jit(solution)/shard_map/slice | solution.py:21
  7.2 13.3 %copy-start.1 = (f32[4,512]{1,0:T(4,128)S(1)}, f32[4,512]{1,0:T(4,128)}, u32[]{:S(2)}) copy-start(f32[4,512]{1,0:T(4,128)} %param.4) | copy-start | bytes 24580
  13.5 3.2 %copy-start = (bf16[32,131072]{1,0:T(8,128)(2,1)}, bf16[32,131072]{1,0:T(8,128)(2,1)S(1)}, u32[]{:S(2)}) copy-start(bf16[32,131072]{1,0:T(8,128)(2,1)S(1)} %convert_element_type.43) | copy-start | bytes 25165828
  16.8 3.7 %collective-permute-start = (bf16[32,1536]{1,0:T(8,128)(2,1)S(1)}, bf16[32,1536]{1,0:T(8,128)(2,1)S(1)}, u32[]{:S(2)}, u32[]{:S(2)}) collective-permute-start(bf16[32,1536]{1,0:T(8,128)(2,1)S(1)} %slice.54), channel_id=1, source_target_pairs={{0,8},{8,16},{16,24},{1,9},{9,17},{17,25},{2,10},{10,18},{18,26},{... | collective-permute-start | bytes 294920 | tf_op jit(solution)/shard_map/ppermute | solution.py:17
  61.5 102.1 %all-to-all-start = ((bf16[8,16,2,32,256]{4,1,3,2,0:T(8,128)(2,1)}), bf16[8,16,2,32,256]{4,1,3,2,0:T(8,128)(2,1)}, u32[]{:S(2)}, u32[]{:S(2)}) async-start(bf16[8,16,2,32,256]{4,1,3,2,0:T(8,128)(2,1)} %get-tuple-element.15), calls=%async_computation | async-start | bytes 8388608 | tf_op jit(solution)/shard_map/all_to_all | solution.py:69
  68.1 112.7 %reduce-scatter.5.cloned.1.call-start = ((), (), s32[]{:S(2)}) async-start(), calls=%async_computation.4 | async-start | bytes 147456 | tf_op jit(solution)/shard_map/reduce_scatter | solution.py:68
  68.8 158.0 %reduce-scatter.3.cloned.1.call-start = ((), (), s32[]{:S(2)}) async-start(), calls=%async_computation.3 | async-start | bytes 5242880 | tf_op jit(solution)/shard_map/reduce_scatter | solution.py:72
Sparse Core Ops, SparseCore 0:
  72.8 107.9 reduce-scatter.4
  183.3 43.5 reduce-scatter.2
where the time goes:
time: 237 us; the launch traced here: 236 us
  waiting for transfers between devices  143 us (60%)
  matrix products  29.5 us (12%)
  local copies, waits for them, and re-layouts  21.9 us (9%)
  other arithmetic  18.5 us (8%)
  between operations  14.2 us (6%)
  starting transfers between devices  9.1 us (4%)
    all_to_all x1, waiting for transfers between devices, on_device(): lax.all_to_all(spectra, 'inp', split_axis=0, concat_axis=3, tiled=True)  94.7 us
    reduce_scatter x1, waiting for transfers between devices, on_device(): visibility = lax.psum_scatter(packed, 'tm', scatter_dimension=0, tiled=True)  44.8 us
    dot_general x1, matrix products, on_device(): jnp.einsum('gcqp,isp->gcqis', table, filtered, preferred_element_type=jnp...  24.7 us
    reshape x1, local copies, waits for them, and re-layouts, on_device(): jnp.concatenate([earlier, volts], axis=1)  9.12 us
    concatenate x1, other arithmetic, on_device(): jnp.concatenate([earlier, volts], axis=1)  7.17 us
    all_to_all x1, starting transfers between devices, on_device(): lax.all_to_all(spectra, 'inp', split_axis=0, concat_axis=3, tiled=True)  6.66 us
    convert_element_type x1, other arithmetic, on_device(): volts = voltage.astype(jnp.bfloat16)  6.34 us
    select_n x1, local copies, waits for them, and re-layouts, packed_rows(): return jnp.where(upper, real_part, imag_part)  5.49 us
  transfers between devices with their start and end apart: 4, of which 3 were waited for; matrix products, arithmetic and copies ran while one was open for 7% of the time, Pallas kernels for 0%

commit v1 on v0

v1 whole, which is shorter than its diff:
```python
import functools
import math

import jax
import jax.numpy as jnp
from jax import lax
from jax.experimental import pallas as pl
from jax.experimental.pallas import tpu as pltpu
from jax.sharding import PartitionSpec as P

P_SIZE = 512
TAPS = 4
NCH = 128
LANES = 128
ROWS = 8
PIECES = P_SIZE // LANES
VMEM_BYTES = 50 * 1024 * 1024
SMALL_BYTES = 20 * 1024 * 1024


def odd_rows(rows):
    tiles = rows // ROWS
    return (tiles + 1 - tiles % 2) * ROWS


def write_table(chan_ref, table):
    chosen = chan_ref[pl.ds(0, 1), :].astype(jnp.float32)
    chosen = jnp.broadcast_to(chosen, (NCH, LANES)).T.astype(jnp.int32)
    factor = 1.0 / math.sqrt(P_SIZE)
    quarter = P_SIZE // 4
    for n in range(PIECES):
        points = lax.broadcasted_iota(jnp.int32, (NCH, LANES), 1) + n * LANES
        phase = (chosen * points) & (P_SIZE - 1)
        turned = phase + quarter // 2
        quadrant = (turned // quarter) & 3
        x = ((turned & (quarter - 1)) - quarter // 2).astype(jnp.float32)
        x = x * (2.0 * math.pi / P_SIZE)
        z = x * x
        sine = x + x * z * (
            -1.6666654611e-1 + z * (8.3321608736e-3 + z * -1.9515295891e-4)
        )
        cosine = 1.0 - 0.5 * z + z * z * (
            4.166664568298827e-2 + z * (-1.388731625493765e-3 + z * 2.443315711809948e-5)
        )
        odd = (quadrant & 1) == 1
        real = jnp.where(odd, sine, cosine)
        imag = jnp.where(odd, cosine, sine)
        real = jnp.where((quadrant == 1) | (quadrant == 2), -real, real)
        imag = jnp.where(quadrant >= 2, imag, -imag)
        at = pl.ds(n * LANES, LANES)
        table[pl.ds(0, NCH), at] = (real * factor).astype(jnp.bfloat16)
        table[pl.ds(NCH, NCH), at] = (imag * factor).astype(jnp.bfloat16)


def channelize_kernel(opening, groups, plan, volts_ref, *refs):
    if opening:
        chan_hbm, taps_hbm, *refs = refs
        *outs, table_ref, tail_ref, taps_ref, chan_ref, held, filt, spec, sems = refs
    else:
        halo_ref, taps_ref, table_ref, *refs = refs
        *outs, held, filt, spec, sems = refs
    blocks, extent = held.shape[0], held.shape[1]
    span = extent - (TAPS - 1)
    inputs = blocks * ROWS
    slots = NCH // groups
    pitch, depth = odd_rows(span), odd_rows(inputs)
    me = lax.axis_index("inp")

    def copy_of(b):
        if opening:
            source = volts_ref.at[b, pl.ds(volts_ref.shape[1] - extent, extent)]
            target = held.at[b]
        else:
            source = volts_ref.at[b, pl.ds(0, span)]
            target = held.at[b, pl.ds(TAPS - 1, span)]
        return pltpu.make_async_copy(source, target, sems.at[b])

    if opening:
        chan_copy = pltpu.make_async_copy(chan_hbm, chan_ref, sems.at[blocks])
        taps_copy = pltpu.make_async_copy(taps_hbm, taps_ref, sems.at[blocks + 1])
        chan_copy.start()
        taps_copy.start()
    for b in range(blocks):
        copy_of(b).start()
    if opening:
        chan_copy.wait()
        write_table(chan_ref, table_ref)
        taps_copy.wait()

    def one_block(b, carry):
        copy_of(b).wait()
        taps = [
            [
                jnp.broadcast_to(taps_ref[pl.ds(k, 1), pl.ds(n * LANES, LANES)], (ROWS, LANES))
                for n in range(PIECES)
            ]
            for k in range(TAPS)
        ]
        if opening:
            for k in range(TAPS - 1):
                for n in range(PIECES):
                    tail_ref[b, k, n] = held[b, span + k, n].astype(jnp.float32)
            before = [
                [held[b, k, n].astype(jnp.float32) for n in range(PIECES)]
                for k in range(TAPS - 1)
            ]
        else:
            before = [[halo_ref[b, k, n] for n in range(PIECES)] for k in range(TAPS - 1)]

        def filter_step(step, window):
            window = [list(w) for w in window]
            for u in range(ROWS):
                s = step * ROWS + u
                now = [held[b, s + TAPS - 1, n].astype(jnp.float32) for n in range(PIECES)]
                window = window + [now]
                for n in range(PIECES):
                    total = taps[0][n] * window[0][n]
                    for k in range(1, TAPS):
                        total = total + taps[k][n] * window[k][n]
                    filt[n, pl.ds(s, ROWS, stride=pitch), :] = total
                window = window[1:]
            return window

        lax.fori_loop(0, span // ROWS, filter_step, before)

        def transform(pair, carry):
            rows = []
            for e in range(2):
                at = pl.ds(pl.multiple_of((pair * 2 + e) * pitch, ROWS), span)
                line = [filt[n, at, :].astype(jnp.bfloat16) for n in range(PIECES)]
                rows.append(jnp.concatenate(line, axis=1))
            out = lax.dot_general(
                table_ref[...],
                jnp.concatenate(rows, axis=0),
                (((1,), (1,)), ((), ())),
                preferred_element_type=jnp.float32,
            )
            for e in range(2):
                i = b * ROWS + pair * 2 + e
                spec[pl.ds(i, 2 * NCH, stride=depth), :] = out[:, e * span : (e + 1) * span]
            return carry

        return lax.fori_loop(0, ROWS // 2, transform, carry)

    lax.fori_loop(0, blocks, one_block, 0)
    for out, pieces in zip(outs, plan):
        count = out.shape[1]
        for place, (j, first) in enumerate(pieces):
            for q in range(2):
                there = j if opening else me ^ j
                start = (q * NCH + there * slots + first) * depth
                rows = spec[pl.ds(pl.multiple_of(start, depth), count * depth), :]
                rows = rows.reshape(count, depth, span)[:, :inputs]
                out[place, :, pl.ds(q * inputs, inputs), :] = rows.astype(jnp.bfloat16)


def channelize(volts, extra, groups, plan, counts):
    opening = len(extra) == 2
    blocks, spectra = volts.shape[:2]
    span = spectra // 2
    inputs = blocks * ROWS
    whole = pl.BlockSpec(memory_space=pltpu.VMEM)
    far = pl.BlockSpec(memory_space=pltpu.HBM)
    out_shape = [
        jax.ShapeDtypeStruct((len(pieces), count, 2 * inputs, span), jnp.bfloat16)
        for pieces, count in zip(plan, counts)
    ]
    scratch = [
        pltpu.VMEM((blocks, span + TAPS - 1, PIECES, ROWS, LANES), jnp.int32),
        pltpu.VMEM((PIECES, ROWS * odd_rows(span), LANES), jnp.float32),
        pltpu.VMEM((2 * NCH * odd_rows(inputs), span), jnp.float32),
        pltpu.SemaphoreType.DMA((blocks + 2,)),
    ]
    if opening:
        out_shape.append(jax.ShapeDtypeStruct((2 * NCH, P_SIZE), jnp.bfloat16))
        out_shape.append(
            jax.ShapeDtypeStruct((blocks, TAPS - 1, PIECES, ROWS, LANES), jnp.float32)
        )
        out_shape.append(jax.ShapeDtypeStruct((TAPS, P_SIZE), jnp.float32))
        scratch = [pltpu.VMEM(extra[0].shape, jnp.int32)] + scratch
    in_specs = [far, far, far] if opening else [far, whole, whole, whole]
    moved = blocks * ROWS * span * P_SIZE * 4 + 2 * NCH * inputs * span * 2
    return pl.pallas_call(
        functools.partial(channelize_kernel, opening, groups, plan),
        out_shape=out_shape,
        in_specs=in_specs,
        out_specs=[whole] * len(out_shape),
        scratch_shapes=scratch,
        compiler_params=pltpu.CompilerParams(vmem_limit_bytes=VMEM_BYTES),
        cost_estimate=pl.CostEstimate(flops=1000, bytes_accessed=12000000, transcendentals=0),
    )(volts, *extra)


def correlate_kernel(groups, others, first, total, places, *refs):
    *parts, beam, stack = refs[-others - 2 :]
    channels = beam.shape[0]
    everyone = parts[0].shape[-1]
    inputs = everyone // groups
    span = beam.shape[1] // 2
    rows_each = everyone // others
    me = lax.axis_index("inp")
    here = lax.axis_index("tm")

    def one_channel(c, carry):
        for j in range(groups):
            at = pl.ds(pl.multiple_of((me ^ j) * inputs, inputs), inputs)
            for h in range(2):
                operand, index, start = (places[j], 0, 0) if h == 0 else (0, me ^ j, first)
                for q in range(2):
                    piece = refs[operand][index, start + c, pl.ds(q * inputs, inputs), :]
                    stack[at, pl.ds((2 * h + q) * span, span)] = piece.astype(stack.dtype)
        values = stack[...].astype(jnp.bfloat16)
        wide = values.astype(jnp.float32)
        power = jnp.sum(wide * wide, axis=0, keepdims=True)
        power = jnp.concatenate(
            [
                power[:, 2 * h * span : (2 * h + 1) * span]
                + power[:, (2 * h + 1) * span : (2 * h + 2) * span]
                for h in range(2)
            ],
            axis=1,
        )
        beam[pl.ds(c, 1), :] = power * (1.0 / everyone)
        col = lax.broadcasted_iota(jnp.int32, (rows_each, everyone), 1)
        row = lax.broadcasted_iota(jnp.int32, (rows_each, everyone), 0)
        for k in range(others):
            base = (here ^ k) * rows_each
            some = stack[pl.ds(pl.multiple_of(base, rows_each), rows_each), :]
            some = some.astype(jnp.bfloat16)
            turned = jnp.concatenate(
                [
                    part
                    for h in range(2)
                    for part in (
                        some[:, (2 * h + 1) * span : (2 * h + 2) * span],
                        -some[:, 2 * h * span : (2 * h + 1) * span],
                    )
                ],
                axis=1,
            )
            both = lax.dot_general(
                jnp.concatenate([some, turned], axis=0),
                values,
                (((1,), (1,)), ((), ())),
                preferred_element_type=jnp.float32,
            )
            packed = jnp.where(row + base <= col, both[:rows_each], both[rows_each:])
            parts[k][c] = (packed * (1.0 / total)).astype(parts[k].dtype)
        return carry

    lax.fori_loop(0, channels, one_channel, 0)


def exchange_order(others):
    order = [0]
    distance = others // 2
    while distance >= 1:
        order = order + [k + distance for k in order]
        distance //= 2
    return order


def correlate(operands, places, groups, first, channels, others, total):
    double, span = operands[0].shape[-2:]
    everyone = double // 2 * groups
    rows_each = everyone // others
    whole = pl.BlockSpec(memory_space=pltpu.VMEM)
    shape = (channels, rows_each, everyone)
    parts = [jax.ShapeDtypeStruct(shape, jnp.float32)]
    parts += [jax.ShapeDtypeStruct(shape, jnp.bfloat16)] * (others - 1)
    held = jnp.bfloat16 if double % 32 == 0 else jnp.float32
    return pl.pallas_call(
        functools.partial(correlate_kernel, groups, others, first, total, places),
        out_shape=parts + [jax.ShapeDtypeStruct((channels, 2 * span), jnp.float32)],
        in_specs=[whole] * len(operands),
        out_specs=[whole] * (others + 1),
        scratch_shapes=[pltpu.VMEM((everyone, 4 * span), held)],
        compiler_params=pltpu.CompilerParams(vmem_limit_bytes=SMALL_BYTES),
        cost_estimate=pl.CostEstimate(flops=1000, bytes_accessed=100000000, transcendentals=0),
    )(*operands)


def finish_kernel(cuts, *refs):
    out = refs[-1]
    for at, (first, count) in enumerate(cuts):
        step = (len(refs) - 1) // len(cuts) - 1
        came = refs[len(cuts) + at * step : len(cuts) + (at + 1) * step]
        for c in range(count):
            total = refs[at][c]
            for part in came:
                total = total + part[c].astype(jnp.float32)
            out[:, first + c, :] = total


def finish(kept, came, cuts):
    rows_each, everyone = kept[0].shape[1:]
    slots = sum(count for _, count in cuts)
    whole = pl.BlockSpec(memory_space=pltpu.VMEM)
    return pl.pallas_call(
        functools.partial(finish_kernel, cuts),
        out_shape=jax.ShapeDtypeStruct((rows_each, slots, everyone), jnp.float32),
        in_specs=[whole] * (len(kept) + len(came)),
        out_specs=whole,
        cost_estimate=pl.CostEstimate(flops=1000, bytes_accessed=1000, transcendentals=0),
        compiler_params=pltpu.CompilerParams(vmem_limit_bytes=SMALL_BYTES),
    )(*kept, *came)


def swapped(block, axis, distance):
    devices = range(lax.axis_size(axis))
    return lax.ppermute(block, axis, [(i, i ^ distance) for i in devices])


def after(block, *earlier):
    if not earlier:
        return block
    return lax.optimization_barrier((block, *earlier))[0]


def send_order(groups):
    half = groups // 2
    return list(range(half, groups)) + list(range(1, half))


def channel_cuts(slots):
    sizes = [8, 8] if slots == 16 else [slots]
    firsts = [sum(sizes[:n]) for n in range(len(sizes))]
    return list(zip(firsts, sizes))


def on_device(voltage, taps, chan_table):
    inputs = voltage.shape[0]
    spectra = voltage.shape[1] // P_SIZE
    groups = lax.axis_size("inp")
    others = lax.axis_size("tm")
    slots = NCH // groups
    total = spectra * others
    cuts = channel_cuts(slots)
    volts = voltage.reshape(inputs // ROWS, ROWS, spectra, PIECES, LANES)
    volts = jnp.transpose(volts, (0, 2, 3, 1, 4))

    plan = [[(d, 0) for d in range(groups)]]
    late, table, tail, taps = channelize(
        volts, (chan_table.reshape(-1, LANES), taps), groups, plan, [slots]
    )
    late = lax.all_to_all(late, "inp", split_axis=0, concat_axis=0, tiled=True)
    devices = range(others)
    halo = lax.ppermute(tail, "tm", [(i - 1, i) for i in devices if i > 0])

    plan, counts = [], []
    for first, count in cuts:
        plan += [[(j, first)] for j in range(groups)]
        counts += [count] * groups
    early = channelize(volts, (halo, taps, table), groups, plan, counts)

    order = send_order(groups)
    kept, came, beams = [], [], []
    for at, (first, count) in enumerate(cuts):
        mine = early[at * groups : (at + 1) * groups]
        got = [swapped(mine[j], "inp", j) for j in order]
        operands = [late, mine[0]] + got
        places = [1] + [2 + order.index(j) for j in range(1, groups)]
        *parts, beam = correlate(operands, places, groups, first, count, others, total)
        kept.append(parts[0])
        came.append([swapped(parts[k], "tm", k) for k in range(1, others)])
        beams.append(beam)
    visibility = finish(kept, sum(came, []), cuts)
    return visibility, jnp.concatenate(beams, axis=0)


def solution(mesh):
    in_specs = (P("inp", "tm"), P(), P())
    out_specs = (P("tm", "inp", None), P("inp", "tm"))
    return jax.shard_map(
        on_device, mesh=mesh, in_specs=in_specs, out_specs=out_specs, check_vma=False
    )
```

time: 237 us -> 139 us (0.59)
  waiting for transfers between devices: 143 us -> 58.2 us
  starting transfers between devices: 9.1 us -> 42.7 us
  matrix products: 29.5 us -> 0 us
  Pallas kernels: 0 us -> 27.9 us
  other arithmetic: 18.5 us -> 0.61 us
  local copies, waits for them, and re-layouts: 21.9 us -> 6.86 us
  between operations: 14.2 us -> 0.78 us
    all_to_all x1, waiting for transfers between devices: 94.7 us -> 0.01 us  [on_device(): late = lax.all_to_all(late, 'inp', split_axis=0, concat_axis=0, tiled=True)]
    ppermute x1 -> x21, waiting for transfers between devices: 0.01 us -> 58.2 us  [the longest x20 57.1 us: swapped(): return lax.ppermute(block, axis, [(i, i ^ distance) for i in devices])]
    reduce_scatter x2 -> x0, waiting for transfers between devices: 47.5 us -> none  [the longest x1 44.8 us: on_device(): visibility = lax.psum_scatter(packed, 'tm', scatter_dimension=0, tiled=True)]
    ppermute x1 -> x21, starting transfers between devices: 2.36 us -> 35.5 us  [the longest x20 34 us: swapped(): return lax.ppermute(block, axis, [(i, i ^ distance) for i in devices])]
    dot_general x3 -> x0, matrix products: 29.5 us -> none  [the longest x1 24.7 us: on_device(): jnp.einsum('gcqp,isp->gcqis', table, filtered, preferred_element_type=jnp...]
    pallas_call x0 -> x5, Pallas kernels: none -> 27.9 us  [the longest x2 17.9 us: channelize(): pl.pallas_call(functools.partial(channelize_kernel, opening, groups, plan...]
    reshape x1 -> x0, local copies, waits for them, and re-layouts: 9.12 us -> none  [on_device(): jnp.concatenate([earlier, volts], axis=1)]
    concatenate x1, other arithmetic: 7.17 us -> 0.61 us  [on_device(): return (visibility, jnp.concatenate(beams, axis=0))]
  transfers between devices with their start and end apart: 4 -> 22, of which waited for: 3 -> 8; matrix products, arithmetic and copies ran while one was open for 7% -> 0% of each run, Pallas kernels for 0% -> 13%
where the time goes in v1:
time: 139 us; the launch traced here: 137 us
  waiting for transfers between devices  58.2 us (42%)
  starting transfers between devices  42.7 us (31%)
  Pallas kernels  27.9 us (20%)
  local copies, waits for them, and re-layouts  6.86 us (5%)
    ppermute x20, waiting for transfers between devices, swapped(): return lax.ppermute(block, axis, [(i, i ^ distance) for i in devices])  57.1 us
    ppermute x20, starting transfers between devices, swapped(): return lax.ppermute(block, axis, [(i, i ^ distance) for i in devices])  34 us
    pallas_call x2, Pallas kernels, channelize(): pl.pallas_call(functools.partial(channelize_kernel, opening, groups, plan...  17.9 us
    pallas_call x2, Pallas kernels, correlate(): pl.pallas_call(functools.partial(correlate_kernel, groups, others, first,...  8.43 us
    all_to_all x1, starting transfers between devices, on_device(): late = lax.all_to_all(late, 'inp', split_axis=0, concat_axis=0, tiled=True)  7.28 us
    unnamed x26, local copies, waits for them, and re-layouts  6.86 us
  transfers between devices with their start and end apart: 22, of which 8 were waited for; matrix products, arithmetic and copies ran while one was open for 0% of the time, Pallas kernels for 13%

profile of v1, /device:TPU:0, one launch (start us, length us, event | category | flops | bytes accessed | tf_op | source)
XLA Modules:
  0.0 137.0 jit_solution(1939152638077534526)
XLA Ops:
  0.6 0.0 copy-start.3
  0.6 0.7 copy-done.3
  1.3 0.7 copy-done.4
  2.0 8.6 %shard_map.50 = (bf16[8,16,64,128]{3,2,1,0:T(8,128)(2,1)S(1)}, bf16[256,512]{1,0:T(8,128)(2,1)S(1)}, f32[4,3,4,8,128]{4,3,2,1,0:T(8,128)S(1)}, f32[4,512]{1,0:T(4,128)S(1)}) custom-call(s32[4,256,4,8,128]{4,3,2,1,0:T(8,128)} %bitcast.5, s32[2,128]{1,0:T(2,128)S(1)} %bitcast.4, f32[4,512]{1,0:T(4,128)S(1)} %copy-done.3), custom_call_target="tpu_custom_call" | custom-call | flops 1000 | bytes 12000000 | tf_op jit(solution)/shard_map/pallas_call | solution.py:183
  10.6 0.0 copy-start
  10.6 1.4 copy-done
  12.0 7.3 %all-to-all-start = ((bf16[8,16,64,128]{3,2,1,0:T(8,128)(2,1)}), bf16[8,16,64,128]{3,2,1,0:T(8,128)(2,1)S(1)}, u32[]{:S(2)}, u32[]{:S(2)}) async-start(bf16[8,16,64,128]{3,2,1,0:T(8,128)(2,1)} %copy-done), calls=%async_computation | async-start | bytes 4194304 | tf_op jit(solution)/shard_map/all_to_all | solution.py:346
  19.2 1.5 %collective-permute-start = (f32[4,3,4,8,128]{4,3,2,1,0:T(8,128)S(1)}, f32[4,3,4,8,128]{4,3,2,1,0:T(8,128)S(1)}, u32[]{:S(2)}, u32[]{:S(2)}) collective-permute-start(f32[4,3,4,8,128]{4,3,2,1,0:T(8,128)S(1)} %get-tuple-element.33), channel_id=1, source_target_pairs={{0,8},{8,16},{16,24},{1,9},{9,17},{17,25},{2,10},{10,18},{18,26},{... | collective-permute-start | bytes 589832 | tf_op jit(solution)/shard_map/ppermute | solution.py:348
  20.7 1.0 collective-permute-done.refs_0_
  21.8 9.3 %shard_map.51 = (bf16[1,8,64,128]{3,2,1,0:T(8,128)(2,1)S(1)}, bf16[1,8,64,128]{3,2,1,0:T(8,128)(2,1)S(1)}, bf16[1,8,64,128]{3,2,1,0:T(8,128)(2,1)S(1)}, bf16[1,8...) custom-call(s32[4,256,4,8,128]{4,3,2,1,0:T(8,128)} %bitcast.6, ...), custom_call_target="tpu_custom_call" | custom-call | flops 1000 | bytes 12000000 | tf_op jit(solution)/shard_map/pallas_call | solution.py:183
  31.0 0.0 copy-start.5
  31.0 0.6 copy-done.5
  31.7 0.6 copy-done.7
  32.3 0.6 copy-done.9
  33.0 0.7 copy-done.11
  33.6 2.8 %collective-permute-start.8 = (bf16[1,8,64,128]{3,2,1,0:T(8,128)(2,1)S(1)}, bf16[1,8,64,128]{3,2,1,0:T(8,128)(2,1)S(1)}, u32[]{:S(2)}, u32[]{:S(2)}) collective-permute-start(bf16[1,8,64,128]{3,2,1,0:T(8,128)(2,1)S(1)} %get-tuple-element.46), channel_id=1, source_target_pairs={{0,4},{1,5},{2,6},{3,7},{4,0},{5,1},{6,2},{7,3},{8,12},{9,13},{10,... | collective-permute-start | bytes 393224 | tf_op jit(solution)/shard_map/ppermute | solution.py:311
  36.4 1.5 %collective-permute-start.9 = (bf16[1,8,64,128]{3,2,1,0:T(8,128)(2,1)S(1)}, bf16[1,8,64,128]{3,2,1,0:T(8,128)(2,1)S(1)}, u32[]{:S(2)}, u32[]{:S(2)}) collective-permute-start(bf16[1,8,64,128]{3,2,1,0:T(8,128)(2,1)S(1)} %get-tuple-element.47), channel_id=1, source_target_pairs={{0,5},{1,4},{2,7},{3,6},{4,1},{5,0},{6,3},{7,2},{8,13},{9,12},{10,... | collective-permute-start | bytes 393224 | tf_op jit(solution)/shard_map/ppermute | solution.py:311
  37.8 3.2 %collective-permute-start.10 = (bf16[1,8,64,128]{3,2,1,0:T(8,128)(2,1)S(1)}, bf16[1,8,64,128]{3,2,1,0:T(8,128)(2,1)S(1)}, u32[]{:S(2)}, u32[]{:S(2)}) collective-permute-start(bf16[1,8,64,128]{3,2,1,0:T(8,128)(2,1)S(1)} %get-tuple-element.48), channel_id=1, source_target_pairs={{0,6},{1,7},{2,4},{3,5},{4,2},{5,3},{6,0},{7,1},{8,14},{9,15},{10,... | collective-permute-start | bytes 393224 | tf_op jit(solution)/shard_map/ppermute | solution.py:311
  41.1 0.2 collective-permute-start.11
  41.3 1.8 %collective-permute-start.12 = (bf16[1,8,64,128]{3,2,1,0:T(8,128)(2,1)S(1)}, bf16[1,8,64,128]{3,2,1,0:T(8,128)(2,1)S(1)}, u32[]{:S(2)}, u32[]{:S(2)}) collective-permute-start(bf16[1,8,64,128]{3,2,1,0:T(8,128)(2,1)S(1)} %get-tuple-element.50), channel_id=1, source_target_pairs={{0,1},{1,0},{2,3},{3,2},{4,5},{5,4},{6,7},{7,6},{8,9},{9,8},{10,11... | collective-permute-start | bytes 393224 | tf_op jit(solution)/shard_map/ppermute | solution.py:311
  43.1 39.8 %collective-permute-done.8.refs_2_ = bf16[1,8,64,128]{3,2,1,0:T(8,128)(2,1)S(1)} collective-permute-done((bf16[1,8,64,128]{3,2,1,0:T(8,128)(2,1)S(1)}, bf16[1,8,64,128]{3,2,1,0:T(8,128)(2,1)S(1)}, u32[]{:S(2)}, u32[]{:S(2)}) %collective-permute-start.8) | collective-permute-done | bytes 131104 | tf_op jit(solution)/shard_map/ppermute | solution.py:311
  82.9 0.0 collective-permute-start.13
  83.0 3.3 %collective-permute-done.9.refs_3_ = bf16[1,8,64,128]{3,2,1,0:T(8,128)(2,1)S(1)} collective-permute-done((bf16[1,8,64,128]{3,2,1,0:T(8,128)(2,1)S(1)}, bf16[1,8,64,128]{3,2,1,0:T(8,128)(2,1)S(1)}, u32[]{:S(2)}, u32[]{:S(2)}) %collective-permute-start.9) | collective-permute-done | bytes 131104 | tf_op jit(solution)/shard_map/ppermute | solution.py:311
  86.3 0.0 collective-permute-start.14
  86.3 0.0 collective-permute-done.10.refs_4_
  86.3 2.3 %collective-permute-start.1 = (bf16[1,8,64,128]{3,2,1,0:T(8,128)(2,1)}, bf16[1,8,64,128]{3,2,1,0:T(8,128)(2,1)S(1)}, u32[]{:S(2)}, u32[]{:S(2)}) collective-permute-start(bf16[1,8,64,128]{3,2,1,0:T(8,128)(2,1)} %get-tuple-element.37), channel_id=1, source_target_pairs={{0,4},{1,5},{2,6},{3,7},{4,0},{5,1},{6,2},{7,3},{8,12},{9,13},{10,... | collective-permute-start | bytes 393224 | tf_op jit(solution)/shard_map/ppermute | solution.py:311
  88.6 0.0 collective-permute-done.11.refs_5_
  88.6 7.9 %collective-permute-start.2 = (bf16[1,8,64,128]{3,2,1,0:T(8,128)(2,1)}, bf16[1,8,64,128]{3,2,1,0:T(8,128)(2,1)S(1)}, u32[]{:S(2)}, u32[]{:S(2)}) collective-permute-start(bf16[1,8,64,128]{3,2,1,0:T(8,128)(2,1)} %get-tuple-element.38), channel_id=1, source_target_pairs={{0,5},{1,4},{2,7},{3,6},{4,1},{5,0},{6,3},{7,2},{8,13},{9,12},{10,... | collective-permute-start | bytes 393224 | tf_op jit(solution)/shard_map/ppermute | solution.py:311
  96.5 0.0 collective-permute-done.12.refs_6_
  96.6 0.0 collective-permute-start.3
  96.6 0.0 collective-permute-done.13.refs_7_
  96.6 0.0 collective-permute-done.14.refs_8_
  96.6 0.0 copy-start.1
  96.6 0.6 copy-done.1
  97.2 0.0 all-to-all-done.refs_0_
  97.2 0.9 copy-done.2
  98.1 4.2 %shard_map.53 = (f32[8,64,256]{2,1,0:T(8,128)S(1)}, bf16[8,64,256]{2,1,0:T(8,128)(2,1)S(1)}, bf16[8,64,256]{2,1,0:T(8,128)(2,1)S(1)}, bf16[8,64,256]{2,1,0:T(8,128)(2,1)S(1)}, f32[8,256]{1,0:T(8,128)S(1)}) custom-call(bf16[8,16,64,128]{3,2,1,0:T(8,128)(2,1)S(1)} %all-to-all-done.refs_0_, bf16[1,8,64,128]{3,2,1,0:T(8,128)(2,1)S(1)} %get-tuple-element.45.refs_1_, ...), custom_call_target="tpu_custom_call" | custom-call | flops 1000 | bytes 100000000 | tf_op jit(solution)/shard_map/pallas_call | solution.py:272
  102.4 0.1 collective-permute-start.18
  102.5 2.2 %collective-permute-start.4 = (bf16[1,8,64,128]{3,2,1,0:T(8,128)(2,1)S(1)}, bf16[1,8,64,128]{3,2,1,0:T(8,128)(2,1)S(1)}, u32[]{:S(2)}, u32[]{:S(2)}) collective-permute-start(bf16[1,8,64,128]{3,2,1,0:T(8,128)(2,1)S(1)} %copy-done.12), channel_id=1, source_target_pairs={{0,7},{1,6},{2,5},{3,4},{4,3},{5,2},{6,1},{7,0},{8,15},{9,14},{10,... | collective-permute-start | bytes 393224 | tf_op jit(solution)/shard_map/ppermute | solution.py:311
  104.7 0.0 collective-permute-done.1.refs_2_
  104.7 3.1 %collective-permute-start.5 = (bf16[1,8,64,128]{3,2,1,0:T(8,128)(2,1)S(1)}, bf16[1,8,64,128]{3,2,1,0:T(8,128)(2,1)S(1)}, u32[]{:S(2)}, u32[]{:S(2)}) collective-permute-start(bf16[1,8,64,128]{3,2,1,0:T(8,128)(2,1)S(1)} %copy-done.10), channel_id=1, source_target_pairs={{0,1},{1,0},{2,3},{3,2},{4,5},{5,4},{6,7},{7,6},{8,9},{9,8},{10,11... | collective-permute-start | bytes 393224 | tf_op jit(solution)/shard_map/ppermute | solution.py:311
  107.8 0.0 collective-permute-done.2.refs_3_
  107.8 0.0 copy-done.8
  107.8 0.0 collective-permute-start.6
  107.8 0.0 collective-permute-done.3.refs_4_
  107.8 4.3 %collective-permute-start.7 = (bf16[1,8,64,128]{3,2,1,0:T(8,128)(2,1)S(1)}, bf16[1,8,64,128]{3,2,1,0:T(8,128)(2,1)S(1)}, u32[]{:S(2)}, u32[]{:S(2)}) collective-permute-start(bf16[1,8,64,128]{3,2,1,0:T(8,128)(2,1)S(1)} %copy-done.6), channel_id=1, source_target_pairs={{0,3},{1,2},{2,1},{3,0},{4,7},{5,6},{6,5},{7,4},{8,11},{9,10},{10,... | collective-permute-start | bytes 393224 | tf_op jit(solution)/shard_map/ppermute | solution.py:311
  112.1 0.0 collective-permute-done.4.refs_5_
  112.1 1.5 %collective-permute-start.19 = (bf16[8,64,256]{2,1,0:T(8,128)(2,1)S(1)}, bf16[8,64,256]{2,1,0:T(8,128)(2,1)S(1)}, u32[]{:S(2)}, u32[]{:S(2)}) collective-permute-start(bf16[8,64,256]{2,1,0:T(8,128)(2,1)S(1)} %get-tuple-element.58), channel_id=1, source_target_pairs={{0,16},{8,24},{16,0},{24,8},{1,17},{9,25},{17,1},{25,9},{2,18},{10... | collective-permute-start | bytes 786440 | tf_op jit(solution)/shard_map/ppermute | solution.py:311
  113.6 0.4 collective-permute-done.5.refs_6_
  114.0 1.1 collective-permute-start.20
  115.2 0.0 collective-permute-done.6.refs_7_
  115.2 1.6 %collective-permute-done.7.refs_8_ = bf16[1,8,64,128]{3,2,1,0:T(8,128)(2,1)S(1)} collective-permute-done((bf16[1,8,64,128]{3,2,1,0:T(8,128)(2,1)S(1)}, bf16[1,8,64,128]{3,2,1,0:T(8,128)(2,1)S(1)}, u32[]{:S(2)}, u32[]{:S(2)}) %collective-permute-start.7) | collective-permute-done | bytes 131104 | tf_op jit(solution)/shard_map/ppermute | solution.py:311
  116.8 4.2 %shard_map.52 = (f32[8,64,256]{2,1,0:T(8,128)S(1)}, bf16[8,64,256]{2,1,0:T(8,128)(2,1)S(1)}, bf16[8,64,256]{2,1,0:T(8,128)(2,1)S(1)}, bf16[8,64,256]{2,1,0:T(8,128)(2,1)S(1)}, f32[8,256]{1,0:T(8,128)S(1)}) custom-call(bf16[8,16,64,128]{3,2,1,0:T(8,128)(2,1)S(1)} %all-to-all-done.refs_0_, bf16[1,8,64,128]{3,2,1,0:T(8,128)(2,1)S(1)} %get-tuple-element.36.refs_1_, ...), custom_call_target="tpu_custom_call" | custom-call | flops 1000 | bytes 100000000 | tf_op jit(solution)/shard_map/pallas_call | solution.py:272
  121.0 0.1 collective-permute-start.15
  121.1 1.5 %collective-permute-start.16 = (bf16[8,64,256]{2,1,0:T(8,128)(2,1)S(1)}, bf16[8,64,256]{2,1,0:T(8,128)(2,1)S(1)}, u32[]{:S(2)}, u32[]{:S(2)}) collective-permute-start(bf16[8,64,256]{2,1,0:T(8,128)(2,1)S(1)} %get-tuple-element.55), channel_id=1, source_target_pairs={{0,16},{8,24},{16,0},{24,8},{1,17},{9,25},{17,1},{25,9},{2,18},{10... | collective-permute-start | bytes 786440 | tf_op jit(solution)/shard_map/ppermute | solution.py:311
  122.6 0.0 collective-permute-done.18.refs_5_
  122.6 0.3 collective-permute-start.17
  122.9 0.6 pad_maximum_fusion
  123.5 0.0 collective-permute-done.19.refs_6_
  123.5 0.4 collective-permute-done.20.refs_7_
  123.9 0.0 collective-permute-done.15.refs_2_
  123.9 6.6 %collective-permute-done.16.refs_3_ = bf16[8,64,256]{2,1,0:T(8,128)(2,1)S(1)} collective-permute-done((bf16[8,64,256]{2,1,0:T(8,128)(2,1)S(1)}, bf16[8,64,256]{2,1,0:T(8,128)(2,1)S(1)}, u32[]{:S(2)}, u32[]{:S(2)}) %collective-permute-start.16) | collective-permute-done | bytes 262176 | tf_op jit(solution)/shard_map/ppermute | solution.py:311
  130.5 4.9 %collective-permute-done.17.refs_4_ = bf16[8,64,256]{2,1,0:T(8,128)(2,1)S(1)} collective-permute-done((bf16[8,64,256]{2,1,0:T(8,128)(2,1)S(1)}, bf16[8,64,256]{2,1,0:T(8,128)(2,1)S(1)}, u32[]{:S(2)}, u32[]{:S(2)}) %collective-permute-start.17) | collective-permute-done | bytes 262176 | tf_op jit(solution)/shard_map/ppermute | solution.py:311
  135.5 1.6 %shard_map.54 = f32[64,16,256]{2,1,0:T(8,128)} custom-call(f32[8,64,256]{2,1,0:T(8,128)S(1)} %get-tuple-element.44.refs_0_, f32[8,64,256]{2,1,0:T(8,128)S(1)} %get-tuple-element.53.refs_1_, bf16[8,64,256]{2,1,0:T(8,128)(2,1)S(1)} %collective-permute-done.15.refs_2_, bf16[8,64,256]{2,1,0:T(8,128)(2,1)S(1)} %collective-permute-done.16.refs_3_, ...), custom_call_target="tpu_custom_call" | custom-call | flops 1000 | bytes 1000 | tf_op jit(solution)/shard_map/pallas_call | solution.py:299
  (12 shorter events, 0.0 us)
Async XLA Ops:
  0.6 0.7 copy-start.3
  1.3 0.7 copy-start.4
  10.6 1.4 copy-start
  12.0 85.3 %all-to-all-start = ((bf16[8,16,64,128]{3,2,1,0:T(8,128)(2,1)}), bf16[8,16,64,128]{3,2,1,0:T(8,128)(2,1)S(1)}, u32[]{:S(2)}, u32[]{:S(2)}) async-start(bf16[8,16,64,128]{3,2,1,0:T(8,128)(2,1)} %copy-done), calls=%async_computation | async-start | bytes 4194304 | tf_op jit(solution)/shard_map/all_to_all | solution.py:346
  19.2 2.5 %collective-permute-start = (f32[4,3,4,8,128]{4,3,2,1,0:T(8,128)S(1)}, f32[4,3,4,8,128]{4,3,2,1,0:T(8,128)S(1)}, u32[]{:S(2)}, u32[]{:S(2)}) collective-permute-start(f32[4,3,4,8,128]{4,3,2,1,0:T(8,128)S(1)} %get-tuple-element.33), channel_id=1, source_target_pairs={{0,8},{8,16},{16,24},{1,9},{9,17},{17,25},{2,10},{10,18},{18,26},{... | collective-permute-start | bytes 589832 | tf_op jit(solution)/shard_map/ppermute | solution.py:348
  31.0 0.6 copy-start.5
  31.7 0.6 copy-start.7
  32.3 0.6 copy-start.9
  33.0 0.7 copy-start.11
  33.6 49.3 %collective-permute-start.8 = (bf16[1,8,64,128]{3,2,1,0:T(8,128)(2,1)S(1)}, bf16[1,8,64,128]{3,2,1,0:T(8,128)(2,1)S(1)}, u32[]{:S(2)}, u32[]{:S(2)}) collective-permute-start(bf16[1,8,64,128]{3,2,1,0:T(8,128)(2,1)S(1)} %get-tuple-element.46), channel_id=1, source_target_pairs={{0,4},{1,5},{2,6},{3,7},{4,0},{5,1},{6,2},{7,3},{8,12},{9,13},{10,... | collective-permute-start | bytes 393224 | tf_op jit(solution)/shard_map/ppermute | solution.py:311
  36.4 49.9 %collective-permute-start.9 = (bf16[1,8,64,128]{3,2,1,0:T(8,128)(2,1)S(1)}, bf16[1,8,64,128]{3,2,1,0:T(8,128)(2,1)S(1)}, u32[]{:S(2)}, u32[]{:S(2)}) collective-permute-start(bf16[1,8,64,128]{3,2,1,0:T(8,128)(2,1)S(1)} %get-tuple-element.47), channel_id=1, source_target_pairs={{0,5},{1,4},{2,7},{3,6},{4,1},{5,0},{6,3},{7,2},{8,13},{9,12},{10,... | collective-permute-start | bytes 393224 | tf_op jit(solution)/shard_map/ppermute | solution.py:311
  37.8 48.5 %collective-permute-start.10 = (bf16[1,8,64,128]{3,2,1,0:T(8,128)(2,1)S(1)}, bf16[1,8,64,128]{3,2,1,0:T(8,128)(2,1)S(1)}, u32[]{:S(2)}, u32[]{:S(2)}) collective-permute-start(bf16[1,8,64,128]{3,2,1,0:T(8,128)(2,1)S(1)} %get-tuple-element.48), channel_id=1, source_target_pairs={{0,6},{1,7},{2,4},{3,5},{4,2},{5,3},{6,0},{7,1},{8,14},{9,15},{10,... | collective-permute-start | bytes 393224 | tf_op jit(solution)/shard_map/ppermute | solution.py:311
  41.1 47.5 %collective-permute-start.11 = (bf16[1,8,64,128]{3,2,1,0:T(8,128)(2,1)S(1)}, bf16[1,8,64,128]{3,2,1,0:T(8,128)(2,1)S(1)}, u32[]{:S(2)}, u32[]{:S(2)}) collective-permute-start(bf16[1,8,64,128]{3,2,1,0:T(8,128)(2,1)S(1)} %get-tuple-element.49), channel_id=1, source_target_pairs={{0,7},{1,6},{2,5},{3,4},{4,3},{5,2},{6,1},{7,0},{8,15},{9,14},{10,... | collective-permute-start | bytes 393224 | tf_op jit(solution)/shard_map/ppermute | solution.py:311
  41.3 55.3 %collective-permute-start.12 = (bf16[1,8,64,128]{3,2,1,0:T(8,128)(2,1)S(1)}, bf16[1,8,64,128]{3,2,1,0:T(8,128)(2,1)S(1)}, u32[]{:S(2)}, u32[]{:S(2)}) collective-permute-start(bf16[1,8,64,128]{3,2,1,0:T(8,128)(2,1)S(1)} %get-tuple-element.50), channel_id=1, source_target_pairs={{0,1},{1,0},{2,3},{3,2},{4,5},{5,4},{6,7},{7,6},{8,9},{9,8},{10,11... | collective-permute-start | bytes 393224 | tf_op jit(solution)/shard_map/ppermute | solution.py:311
  82.9 13.6 %collective-permute-start.13 = (bf16[1,8,64,128]{3,2,1,0:T(8,128)(2,1)S(1)}, bf16[1,8,64,128]{3,2,1,0:T(8,128)(2,1)S(1)}, u32[]{:S(2)}, u32[]{:S(2)}) collective-permute-start(bf16[1,8,64,128]{3,2,1,0:T(8,128)(2,1)S(1)} %get-tuple-element.51), channel_id=1, source_target_pairs={{0,2},{1,3},{2,0},{3,1},{4,6},{5,7},{6,4},{7,5},{8,10},{9,11},{10,... | collective-permute-start | bytes 393224 | tf_op jit(solution)/shard_map/ppermute | solution.py:311
  86.3 10.3 %collective-permute-start.14 = (bf16[1,8,64,128]{3,2,1,0:T(8,128)(2,1)S(1)}, bf16[1,8,64,128]{3,2,1,0:T(8,128)(2,1)S(1)}, u32[]{:S(2)}, u32[]{:S(2)}) collective-permute-start(bf16[1,8,64,128]{3,2,1,0:T(8,128)(2,1)S(1)} %get-tuple-element.52), channel_id=1, source_target_pairs={{0,3},{1,2},{2,1},{3,0},{4,7},{5,6},{6,5},{7,4},{8,11},{9,10},{10,... | collective-permute-start | bytes 393224 | tf_op jit(solution)/shard_map/ppermute | solution.py:311
  86.3 18.4 %collective-permute-start.1 = (bf16[1,8,64,128]{3,2,1,0:T(8,128)(2,1)}, bf16[1,8,64,128]{3,2,1,0:T(8,128)(2,1)S(1)}, u32[]{:S(2)}, u32[]{:S(2)}) collective-permute-start(bf16[1,8,64,128]{3,2,1,0:T(8,128)(2,1)} %get-tuple-element.37), channel_id=1, source_target_pairs={{0,4},{1,5},{2,6},{3,7},{4,0},{5,1},{6,2},{7,3},{8,12},{9,13},{10,... | collective-permute-start | bytes 393224 | tf_op jit(solution)/shard_map/ppermute | solution.py:311
  88.6 19.2 %collective-permute-start.2 = (bf16[1,8,64,128]{3,2,1,0:T(8,128)(2,1)}, bf16[1,8,64,128]{3,2,1,0:T(8,128)(2,1)S(1)}, u32[]{:S(2)}, u32[]{:S(2)}) collective-permute-start(bf16[1,8,64,128]{3,2,1,0:T(8,128)(2,1)} %get-tuple-element.38), channel_id=1, source_target_pairs={{0,5},{1,4},{2,7},{3,6},{4,1},{5,0},{6,3},{7,2},{8,13},{9,12},{10,... | collective-permute-start | bytes 393224 | tf_op jit(solution)/shard_map/ppermute | solution.py:311
  96.6 11.3 %collective-permute-start.3 = (bf16[1,8,64,128]{3,2,1,0:T(8,128)(2,1)}, bf16[1,8,64,128]{3,2,1,0:T(8,128)(2,1)S(1)}, u32[]{:S(2)}, u32[]{:S(2)}) collective-permute-start(bf16[1,8,64,128]{3,2,1,0:T(8,128)(2,1)} %get-tuple-element.39), channel_id=1, source_target_pairs={{0,6},{1,7},{2,4},{3,5},{4,2},{5,3},{6,0},{7,1},{8,14},{9,15},{10,... | collective-permute-start | bytes 393224 | tf_op jit(solution)/shard_map/ppermute | solution.py:311
  96.6 0.6 copy-start.1
  97.2 0.9 copy-start.2
  98.1 4.3 %copy-start.12 = (bf16[1,8,64,128]{3,2,1,0:T(8,128)(2,1)S(1)}, bf16[1,8,64,128]{3,2,1,0:T(8,128)(2,1)}, u32[]{:S(2)}) copy-start(bf16[1,8,64,128]{3,2,1,0:T(8,128)(2,1)} %copy-done.11) | copy-start | bytes 393220
  98.1 6.6 %copy-start.10 = (bf16[1,8,64,128]{3,2,1,0:T(8,128)(2,1)S(1)}, bf16[1,8,64,128]{3,2,1,0:T(8,128)(2,1)}, u32[]{:S(2)}) copy-start(bf16[1,8,64,128]{3,2,1,0:T(8,128)(2,1)} %copy-done.9) | copy-start | bytes 393220
  98.1 9.7 %copy-start.8 = (bf16[1,8,64,128]{3,2,1,0:T(8,128)(2,1)S(1)}, bf16[1,8,64,128]{3,2,1,0:T(8,128)(2,1)}, u32[]{:S(2)}) copy-start(bf16[1,8,64,128]{3,2,1,0:T(8,128)(2,1)} %copy-done.7) | copy-start | bytes 393220
  98.1 9.7 %copy-start.6 = (bf16[1,8,64,128]{3,2,1,0:T(8,128)(2,1)S(1)}, bf16[1,8,64,128]{3,2,1,0:T(8,128)(2,1)}, u32[]{:S(2)}) copy-start(bf16[1,8,64,128]{3,2,1,0:T(8,128)(2,1)} %copy-done.5) | copy-start | bytes 393220
  102.4 20.3 %collective-permute-start.18 = (bf16[8,64,256]{2,1,0:T(8,128)(2,1)S(1)}, bf16[8,64,256]{2,1,0:T(8,128)(2,1)S(1)}, u32[]{:S(2)}, u32[]{:S(2)}) collective-permute-start(bf16[8,64,256]{2,1,0:T(8,128)(2,1)S(1)} %get-tuple-element.57), channel_id=1, source_target_pairs={{0,8},{8,0},{16,24},{24,16},{1,9},{9,1},{17,25},{25,17},{2,10},{10... | collective-permute-start | bytes 786440 | tf_op jit(solution)/shard_map/ppermute | solution.py:311
  102.5 9.7 %collective-permute-start.4 = (bf16[1,8,64,128]{3,2,1,0:T(8,128)(2,1)S(1)}, bf16[1,8,64,128]{3,2,1,0:T(8,128)(2,1)S(1)}, u32[]{:S(2)}, u32[]{:S(2)}) collective-permute-start(bf16[1,8,64,128]{3,2,1,0:T(8,128)(2,1)S(1)} %copy-done.12), channel_id=1, source_target_pairs={{0,7},{1,6},{2,5},{3,4},{4,3},{5,2},{6,1},{7,0},{8,15},{9,14},{10,... | collective-permute-start | bytes 393224 | tf_op jit(solution)/shard_map/ppermute | solution.py:311
  104.7 9.4 %collective-permute-start.5 = (bf16[1,8,64,128]{3,2,1,0:T(8,128)(2,1)S(1)}, bf16[1,8,64,128]{3,2,1,0:T(8,128)(2,1)S(1)}, u32[]{:S(2)}, u32[]{:S(2)}) collective-permute-start(bf16[1,8,64,128]{3,2,1,0:T(8,128)(2,1)S(1)} %copy-done.10), channel_id=1, source_target_pairs={{0,1},{1,0},{2,3},{3,2},{4,5},{5,4},{6,7},{7,6},{8,9},{9,8},{10,11... | collective-permute-start | bytes 393224 | tf_op jit(solution)/shard_map/ppermute | solution.py:311
  107.8 7.3 %collective-permute-start.6 = (bf16[1,8,64,128]{3,2,1,0:T(8,128)(2,1)S(1)}, bf16[1,8,64,128]{3,2,1,0:T(8,128)(2,1)S(1)}, u32[]{:S(2)}, u32[]{:S(2)}) collective-permute-start(bf16[1,8,64,128]{3,2,1,0:T(8,128)(2,1)S(1)} %copy-done.8), channel_id=1, source_target_pairs={{0,2},{1,3},{2,0},{3,1},{4,6},{5,7},{6,4},{7,5},{8,10},{9,11},{10,... | collective-permute-start | bytes 393224 | tf_op jit(solution)/shard_map/ppermute | solution.py:311
  107.8 8.9 %collective-permute-start.7 = (bf16[1,8,64,128]{3,2,1,0:T(8,128)(2,1)S(1)}, bf16[1,8,64,128]{3,2,1,0:T(8,128)(2,1)S(1)}, u32[]{:S(2)}, u32[]{:S(2)}) collective-permute-start(bf16[1,8,64,128]{3,2,1,0:T(8,128)(2,1)S(1)} %copy-done.6), channel_id=1, source_target_pairs={{0,3},{1,2},{2,1},{3,0},{4,7},{5,6},{6,5},{7,4},{8,11},{9,10},{10,... | collective-permute-start | bytes 393224 | tf_op jit(solution)/shard_map/ppermute | solution.py:311
  112.1 11.4 %collective-permute-start.19 = (bf16[8,64,256]{2,1,0:T(8,128)(2,1)S(1)}, bf16[8,64,256]{2,1,0:T(8,128)(2,1)S(1)}, u32[]{:S(2)}, u32[]{:S(2)}) collective-permute-start(bf16[8,64,256]{2,1,0:T(8,128)(2,1)S(1)} %get-tuple-element.58), channel_id=1, source_target_pairs={{0,16},{8,24},{16,0},{24,8},{1,17},{9,25},{17,1},{25,9},{2,18},{10... | collective-permute-start | bytes 786440 | tf_op jit(solution)/shard_map/ppermute | solution.py:311
  114.0 9.9 %collective-permute-start.20 = (bf16[8,64,256]{2,1,0:T(8,128)(2,1)S(1)}, bf16[8,64,256]{2,1,0:T(8,128)(2,1)S(1)}, u32[]{:S(2)}, u32[]{:S(2)}) collective-permute-start(bf16[8,64,256]{2,1,0:T(8,128)(2,1)S(1)} %get-tuple-element.59), channel_id=1, source_target_pairs={{0,24},{8,16},{16,8},{24,0},{1,25},{9,17},{17,9},{25,1},{2,26},{10... | collective-permute-start | bytes 786440 | tf_op jit(solution)/shard_map/ppermute | solution.py:311
  121.0 2.9 %collective-permute-start.15 = (bf16[8,64,256]{2,1,0:T(8,128)(2,1)S(1)}, bf16[8,64,256]{2,1,0:T(8,128)(2,1)S(1)}, u32[]{:S(2)}, u32[]{:S(2)}) collective-permute-start(bf16[8,64,256]{2,1,0:T(8,128)(2,1)S(1)} %get-tuple-element.54), channel_id=1, source_target_pairs={{0,8},{8,0},{16,24},{24,16},{1,9},{9,1},{17,25},{25,17},{2,10},{10... | collective-permute-start | bytes 786440 | tf_op jit(solution)/shard_map/ppermute | solution.py:311
  121.1 9.4 %collective-permute-start.16 = (bf16[8,64,256]{2,1,0:T(8,128)(2,1)S(1)}, bf16[8,64,256]{2,1,0:T(8,128)(2,1)S(1)}, u32[]{:S(2)}, u32[]{:S(2)}) collective-permute-start(bf16[8,64,256]{2,1,0:T(8,128)(2,1)S(1)} %get-tuple-element.55), channel_id=1, source_target_pairs={{0,16},{8,24},{16,0},{24,8},{1,17},{9,25},{17,1},{25,9},{2,18},{10... | collective-permute-start | bytes 786440 | tf_op jit(solution)/shard_map/ppermute | solution.py:311
  122.6 12.8 %collective-permute-start.17 = (bf16[8,64,256]{2,1,0:T(8,128)(2,1)S(1)}, bf16[8,64,256]{2,1,0:T(8,128)(2,1)S(1)}, u32[]{:S(2)}, u32[]{:S(2)}) collective-permute-start(bf16[8,64,256]{2,1,0:T(8,128)(2,1)S(1)} %get-tuple-element.56), channel_id=1, source_target_pairs={{0,24},{8,16},{16,8},{24,0},{1,25},{9,17},{17,9},{25,1},{2,26},{10... | collective-permute-start | bytes 786440 | tf_op jit(solution)/shard_map/ppermute | solution.py:311

commit v2 on v1

--- a/solution.py
+++ b/solution.py
@@ -14,7 +14,7 @@
 LANES = 128
 ROWS = 8
 PIECES = P_SIZE // LANES
-VMEM_BYTES = 50 * 1024 * 1024
+VMEM_BYTES = 62 * 1024 * 1024
 SMALL_BYTES = 20 * 1024 * 1024
 
 
@@ -192,7 +192,7 @@
 
 
 def correlate_kernel(groups, others, first, total, places, *refs):
-    *parts, beam, stack = refs[-others - 2 :]
+    *parts, beam, stack, both = refs[-others - 3 :]
     channels = beam.shape[0]
     everyone = parts[0].shape[-1]
     inputs = everyone // groups
@@ -221,30 +221,30 @@
             axis=1,
         )
         beam[pl.ds(c, 1), :] = power * (1.0 / everyone)
+        turned = jnp.concatenate(
+            [
+                part
+                for h in range(2)
+                for part in (
+                    values[:, (2 * h + 1) * span : (2 * h + 2) * span],
+                    -values[:, 2 * h * span : (2 * h + 1) * span],
+                )
+            ],
+            axis=1,
+        )
+        both[...] = lax.dot_general(
+            jnp.concatenate([values, turned], axis=0),
+            values,
+            (((1,), (1,)), ((), ())),
+            preferred_element_type=jnp.float32,
+        )
         col = lax.broadcasted_iota(jnp.int32, (rows_each, everyone), 1)
         row = lax.broadcasted_iota(jnp.int32, (rows_each, everyone), 0)
         for k in range(others):
-            base = (here ^ k) * rows_each
-            some = stack[pl.ds(pl.multiple_of(base, rows_each), rows_each), :]
-            some = some.astype(jnp.bfloat16)
-            turned = jnp.concatenate(
-                [
-                    part
-                    for h in range(2)
-                    for part in (
-                        some[:, (2 * h + 1) * span : (2 * h + 2) * span],
-                        -some[:, 2 * h * span : (2 * h + 1) * span],
-                    )
-                ],
-                axis=1,
-            )
-            both = lax.dot_general(
-                jnp.concatenate([some, turned], axis=0),
-                values,
-                (((1,), (1,)), ((), ())),
-                preferred_element_type=jnp.float32,
-            )
-            packed = jnp.where(row + base <= col, both[:rows_each], both[rows_each:])
+            base = pl.multiple_of((here ^ k) * rows_each, rows_each)
+            real = both[pl.ds(base, rows_each), :]
+            imag = both[pl.ds(everyone + base, rows_each), :]
+            packed = jnp.where(row + base <= col, real, imag)
             parts[k][c] = (packed * (1.0 / total)).astype(parts[k].dtype)
         return carry
 
@@ -274,7 +274,10 @@
         out_shape=parts + [jax.ShapeDtypeStruct((channels, 2 * span), jnp.float32)],
         in_specs=[whole] * len(operands),
         out_specs=[whole] * (others + 1),
-        scratch_shapes=[pltpu.VMEM((everyone, 4 * span), held)],
+        scratch_shapes=[
+            pltpu.VMEM((everyone, 4 * span), held),
+            pltpu.VMEM((2 * everyone, everyone), jnp.float32),
+        ],
         compiler_params=pltpu.CompilerParams(vmem_limit_bytes=SMALL_BYTES),
         cost_estimate=pl.CostEstimate(flops=1000, bytes_accessed=100000000, transcendentals=0),
     )(*operands)
@@ -362,7 +365,7 @@
         places = [1] + [2 + order.index(j) for j in range(1, groups)]
         *parts, beam = correlate(operands, places, groups, first, count, others, total)
         kept.append(parts[0])
-        came.append([swapped(parts[k], "tm", k) for k in range(1, others)])
+        came.append([swapped(parts[k], "tm", k) for k in reversed(range(1, others))])
         beams.append(beam)
     visibility = finish(kept, sum(came, []), cuts)
     return visibility, jnp.concatenate(beams, axis=0)

time: 139 us -> 136 us (0.978); the launches traced: 137 us -> 136 us
  local copies, waits for them, and re-layouts: 6.86 us -> 1.59 us
  Pallas kernels: 27.9 us -> 32.6 us
    unnamed x26 -> x16, local copies, waits for them, and re-layouts: 6.86 us -> 1.59 us
    pallas_call x2, Pallas kernels: 17.9 us -> 20.9 us  [channelize(): pl.pallas_call(functools.partial(channelize_kernel, opening, groups, plan...]
    pallas_call x2, Pallas kernels: 8.43 us -> 10.1 us  [correlate(): pl.pallas_call(functools.partial(correlate_kernel, groups, others, first,...]
  transfers between devices with their start and end apart: 22 -> 22, of which waited for: 8 -> 7; matrix products, arithmetic and copies ran while one was open for 0% -> 0% of each run, Pallas kernels for 13% -> 15%
where the time goes in v2:
time: 136 us
  waiting for transfers between devices  58.8 us (43%)
  starting transfers between devices  41.6 us (31%)
  Pallas kernels  32.6 us (24%)
  local copies, waits for them, and re-layouts  1.59 us (1%)
    ppermute x20, waiting for transfers between devices, swapped(): return lax.ppermute(block, axis, [(i, i ^ distance) for i in devices])  57.8 us
    ppermute x20, starting transfers between devices, swapped(): return lax.ppermute(block, axis, [(i, i ^ distance) for i in devices])  32.7 us
    pallas_call x2, Pallas kernels, channelize(): pl.pallas_call(functools.partial(channelize_kernel, opening, groups, plan...  20.9 us
    pallas_call x2, Pallas kernels, correlate(): pl.pallas_call(functools.partial(correlate_kernel, groups, others, first,...  10.1 us
    all_to_all x1, starting transfers between devices, on_device(): late = lax.all_to_all(late, 'inp', split_axis=0, concat_axis=0, tiled=True)  7.43 us
  transfers between devices with their start and end apart: 22, of which 7 were waited for; matrix products, arithmetic and copies ran while one was open for 0% of the time, Pallas kernels for 15%

profile of v2, /device:TPU:0, one launch (start us, length us, event | category | flops | bytes accessed | tf_op | source)
XLA Modules:
  0.0 136.0 jit_solution(6176959645682403312)
XLA Ops:
  0.6 10.0 %shard_map.50 = (bf16[8,16,64,128]{3,2,1,0:T(8,128)(2,1)}, bf16[256,512]{1,0:T(8,128)(2,1)}, f32[4,3,4,8,128]{4,3,2,1,0:T(8,128)}, f32[4,512]{1,0:T(4,128)}) custom-call(s32[4,256,4,8,128]{4,3,2,1,0:T(8,128)} %bitcast.4, s32[2,128]{1,0:T(2,128)} %bitcast.6, f32[4,512]{1,0:T(4,128)} %refs_1_.1), custom_call_target="tpu_custom_call" | custom-call | flops 1000 | bytes 12000000 | tf_op jit(solution)/shard_map/pallas_call | solution.py:183
  10.6 0.0 copy-start.3
  10.6 7.4 %all-to-all-start = ((bf16[8,16,64,128]{3,2,1,0:T(8,128)(2,1)}), bf16[8,16,64,128]{3,2,1,0:T(8,128)(2,1)}, u32[]{:S(2)}, u32[]{:S(2)}) async-start(bf16[8,16,64,128]{3,2,1,0:T(8,128)(2,1)} %get-tuple-element.32), calls=%async_computation | async-start | bytes 4194304 | tf_op jit(solution)/shard_map/all_to_all | solution.py:349
  18.0 0.0 copy-done.3
  18.0 1.5 %collective-permute-start = (f32[4,3,4,8,128]{4,3,2,1,0:T(8,128)S(1)}, f32[4,3,4,8,128]{4,3,2,1,0:T(8,128)S(1)}, u32[]{:S(2)}, u32[]{:S(2)}) collective-permute-start(f32[4,3,4,8,128]{4,3,2,1,0:T(8,128)S(1)} %copy-done.3), channel_id=1, source_target_pairs={{0,8},{8,16},{16,24},{1,9},{9,17},{17,25},{2,10},{10,18},{18,26},{... | collective-permute-start | bytes 589832 | tf_op jit(solution)/shard_map/ppermute | solution.py:351
  19.5 1.0 collective-permute-done.refs_0_
  20.6 0.0 copy-start.2
  20.6 0.7 copy-done.2
  21.2 11.0 %shard_map.51 = (bf16[1,8,64,128]{3,2,1,0:T(8,128)(2,1)}, bf16[1,8,64,128]{3,2,1,0:T(8,128)(2,1)}, bf16[1,8,64,128]{3,2,1,0:T(8,128)(2,1)}, bf16[1,8,64,128]{3,2...) custom-call(s32[4,256,4,8,128]{4,3,2,1,0:T(8,128)} %bitcast.5, ...), custom_call_target="tpu_custom_call" | custom-call | flops 1000 | bytes 12000000 | tf_op jit(solution)/shard_map/pallas_call | solution.py:183
  32.2 0.0 copy-start
  32.2 2.8 %collective-permute-start.8 = (bf16[1,8,64,128]{3,2,1,0:T(8,128)(2,1)}, bf16[1,8,64,128]{3,2,1,0:T(8,128)(2,1)S(1)}, u32[]{:S(2)}, u32[]{:S(2)}) collective-permute-start(bf16[1,8,64,128]{3,2,1,0:T(8,128)(2,1)} %get-tuple-element.46), channel_id=1, source_target_pairs={{0,4},{1,5},{2,6},{3,7},{4,0},{5,1},{6,2},{7,3},{8,12},{9,13},{10,... | collective-permute-start | bytes 393224 | tf_op jit(solution)/shard_map/ppermute | solution.py:314
  35.0 1.5 %collective-permute-start.9 = (bf16[1,8,64,128]{3,2,1,0:T(8,128)(2,1)}, bf16[1,8,64,128]{3,2,1,0:T(8,128)(2,1)S(1)}, u32[]{:S(2)}, u32[]{:S(2)}) collective-permute-start(bf16[1,8,64,128]{3,2,1,0:T(8,128)(2,1)} %get-tuple-element.47), channel_id=1, source_target_pairs={{0,5},{1,4},{2,7},{3,6},{4,1},{5,0},{6,3},{7,2},{8,13},{9,12},{10,... | collective-permute-start | bytes 393224 | tf_op jit(solution)/shard_map/ppermute | solution.py:314
  36.5 3.2 %collective-permute-start.10 = (bf16[1,8,64,128]{3,2,1,0:T(8,128)(2,1)}, bf16[1,8,64,128]{3,2,1,0:T(8,128)(2,1)S(1)}, u32[]{:S(2)}, u32[]{:S(2)}) collective-permute-start(bf16[1,8,64,128]{3,2,1,0:T(8,128)(2,1)} %get-tuple-element.48), channel_id=1, source_target_pairs={{0,6},{1,7},{2,4},{3,5},{4,2},{5,3},{6,0},{7,1},{8,14},{9,15},{10,... | collective-permute-start | bytes 393224 | tf_op jit(solution)/shard_map/ppermute | solution.py:314
  39.7 0.2 collective-permute-start.11
  39.9 1.8 %collective-permute-start.12 = (bf16[1,8,64,128]{3,2,1,0:T(8,128)(2,1)}, bf16[1,8,64,128]{3,2,1,0:T(8,128)(2,1)S(1)}, u32[]{:S(2)}, u32[]{:S(2)}) collective-permute-start(bf16[1,8,64,128]{3,2,1,0:T(8,128)(2,1)} %get-tuple-element.50), channel_id=1, source_target_pairs={{0,1},{1,0},{2,3},{3,2},{4,5},{5,4},{6,7},{7,6},{8,9},{9,8},{10,11... | collective-permute-start | bytes 393224 | tf_op jit(solution)/shard_map/ppermute | solution.py:314
  41.8 40.0 %collective-permute-done.8.refs_2_ = bf16[1,8,64,128]{3,2,1,0:T(8,128)(2,1)S(1)} collective-permute-done((bf16[1,8,64,128]{3,2,1,0:T(8,128)(2,1)}, bf16[1,8,64,128]{3,2,1,0:T(8,128)(2,1)S(1)}, u32[]{:S(2)}, u32[]{:S(2)}) %collective-permute-start.8) | collective-permute-done | bytes 131104 | tf_op jit(solution)/shard_map/ppermute | solution.py:314
  81.7 0.0 collective-permute-start.13
  81.7 3.3 %collective-permute-done.9.refs_3_ = bf16[1,8,64,128]{3,2,1,0:T(8,128)(2,1)S(1)} collective-permute-done((bf16[1,8,64,128]{3,2,1,0:T(8,128)(2,1)}, bf16[1,8,64,128]{3,2,1,0:T(8,128)(2,1)S(1)}, u32[]{:S(2)}, u32[]{:S(2)}) %collective-permute-start.9) | collective-permute-done | bytes 131104 | tf_op jit(solution)/shard_map/ppermute | solution.py:314
  85.1 0.0 collective-permute-start.14
  85.1 0.0 collective-permute-done.10.refs_4_
  85.1 2.3 %collective-permute-start.1 = (bf16[1,8,64,128]{3,2,1,0:T(8,128)(2,1)}, bf16[1,8,64,128]{3,2,1,0:T(8,128)(2,1)S(1)}, u32[]{:S(2)}, u32[]{:S(2)}) collective-permute-start(bf16[1,8,64,128]{3,2,1,0:T(8,128)(2,1)} %get-tuple-element.37), channel_id=1, source_target_pairs={{0,4},{1,5},{2,6},{3,7},{4,0},{5,1},{6,2},{7,3},{8,12},{9,13},{10,... | collective-permute-start | bytes 393224 | tf_op jit(solution)/shard_map/ppermute | solution.py:314
  87.4 0.0 collective-permute-done.11.refs_5_
  87.4 6.2 %collective-permute-start.2 = (bf16[1,8,64,128]{3,2,1,0:T(8,128)(2,1)}, bf16[1,8,64,128]{3,2,1,0:T(8,128)(2,1)S(1)}, u32[]{:S(2)}, u32[]{:S(2)}) collective-permute-start(bf16[1,8,64,128]{3,2,1,0:T(8,128)(2,1)} %get-tuple-element.38), channel_id=1, source_target_pairs={{0,5},{1,4},{2,7},{3,6},{4,1},{5,0},{6,3},{7,2},{8,13},{9,12},{10,... | collective-permute-start | bytes 393224 | tf_op jit(solution)/shard_map/ppermute | solution.py:314
  93.6 0.0 collective-permute-done.12.refs_6_
  93.7 0.5 collective-permute-start.3
  94.1 0.0 collective-permute-done.13.refs_7_
  94.1 0.0 collective-permute-done.14.refs_8_
  94.1 0.0 all-to-all-done.refs_0_
  94.1 0.0 copy-start.1
  94.1 0.9 copy-done.1
  95.0 0.0 copy-start.7
  95.0 0.0 copy-start.6
  95.0 5.1 %shard_map.53 = (f32[8,64,256]{2,1,0:T(8,128)S(1)}, bf16[8,64,256]{2,1,0:T(8,128)(2,1)S(1)}, bf16[8,64,256]{2,1,0:T(8,128)(2,1)S(1)}, bf16[8,64,256]{2,1,0:T(8,128)(2,1)S(1)}, f32[8,256]{1,0:T(8,128)S(1)}) custom-call(bf16[8,16,64,128]{3,2,1,0:T(8,128)(2,1)} %all-to-all-done.refs_0_, bf16[1,8,64,128]{3,2,1,0:T(8,128)(2,1)S(1)} %copy-done.1, ...), custom_call_target="tpu_custom_call" | custom-call | flops 1000 | bytes 100000000 | tf_op jit(solution)/shard_map/pallas_call | solution.py:272
  100.1 0.2 collective-permute-start.18
  100.3 0.0 copy-done.7
  100.3 3.2 %collective-permute-start.4 = (bf16[1,8,64,128]{3,2,1,0:T(8,128)(2,1)S(1)}, bf16[1,8,64,128]{3,2,1,0:T(8,128)(2,1)S(1)}, u32[]{:S(2)}, u32[]{:S(2)}) collective-permute-start(bf16[1,8,64,128]{3,2,1,0:T(8,128)(2,1)S(1)} %copy-done.7), channel_id=1, source_target_pairs={{0,7},{1,6},{2,5},{3,4},{4,3},{5,2},{6,1},{7,0},{8,15},{9,14},{10,... | collective-permute-start | bytes 393224 | tf_op jit(solution)/shard_map/ppermute | solution.py:314
  103.5 0.0 collective-permute-done.1.refs_2_
  103.5 0.0 copy-done.6
  103.5 1.8 %collective-permute-start.5 = (bf16[1,8,64,128]{3,2,1,0:T(8,128)(2,1)S(1)}, bf16[1,8,64,128]{3,2,1,0:T(8,128)(2,1)S(1)}, u32[]{:S(2)}, u32[]{:S(2)}) collective-permute-start(bf16[1,8,64,128]{3,2,1,0:T(8,128)(2,1)S(1)} %copy-done.6), channel_id=1, source_target_pairs={{0,1},{1,0},{2,3},{3,2},{4,5},{5,4},{6,7},{7,6},{8,9},{9,8},{10,11... | collective-permute-start | bytes 393224 | tf_op jit(solution)/shard_map/ppermute | solution.py:314
  105.3 0.0 collective-permute-done.2.refs_3_
  105.3 0.0 copy-done.5
  105.3 0.0 collective-permute-start.6
  105.3 0.0 collective-permute-done.3.refs_4_
  105.3 0.0 copy-done.4
  105.3 5.6 %collective-permute-start.7 = (bf16[1,8,64,128]{3,2,1,0:T(8,128)(2,1)S(1)}, bf16[1,8,64,128]{3,2,1,0:T(8,128)(2,1)S(1)}, u32[]{:S(2)}, u32[]{:S(2)}) collective-permute-start(bf16[1,8,64,128]{3,2,1,0:T(8,128)(2,1)S(1)} %copy-done.4), channel_id=1, source_target_pairs={{0,3},{1,2},{2,1},{3,0},{4,7},{5,6},{6,5},{7,4},{8,11},{9,10},{10,... | collective-permute-start | bytes 393224 | tf_op jit(solution)/shard_map/ppermute | solution.py:314
  110.9 0.0 collective-permute-done.4.refs_5_
  110.9 1.5 %collective-permute-start.19 = (bf16[8,64,256]{2,1,0:T(8,128)(2,1)S(1)}, bf16[8,64,256]{2,1,0:T(8,128)(2,1)S(1)}, u32[]{:S(2)}, u32[]{:S(2)}) collective-permute-start(bf16[8,64,256]{2,1,0:T(8,128)(2,1)S(1)} %get-tuple-element.58), channel_id=1, source_target_pairs={{0,16},{8,24},{16,0},{24,8},{1,17},{9,25},{17,1},{25,9},{2,18},{10... | collective-permute-start | bytes 786440 | tf_op jit(solution)/shard_map/ppermute | solution.py:314
  112.4 0.0 collective-permute-done.5.refs_6_
  112.4 0.0 collective-permute-start.20
  112.4 0.1 collective-permute-done.6.refs_7_
  112.5 2.6 %collective-permute-done.7.refs_8_ = bf16[1,8,64,128]{3,2,1,0:T(8,128)(2,1)S(1)} collective-permute-done((bf16[1,8,64,128]{3,2,1,0:T(8,128)(2,1)S(1)}, bf16[1,8,64,128]{3,2,1,0:T(8,128)(2,1)S(1)}, u32[]{:S(2)}, u32[]{:S(2)}) %collective-permute-start.7) | collective-permute-done | bytes 131104 | tf_op jit(solution)/shard_map/ppermute | solution.py:314
  115.1 0.0 copy-done
  115.1 5.0 %shard_map.52 = (f32[8,64,256]{2,1,0:T(8,128)S(1)}, bf16[8,64,256]{2,1,0:T(8,128)(2,1)S(1)}, bf16[8,64,256]{2,1,0:T(8,128)(2,1)S(1)}, bf16[8,64,256]{2,1,0:T(8,128)(2,1)S(1)}, f32[8,256]{1,0:T(8,128)S(1)}) custom-call(bf16[8,16,64,128]{3,2,1,0:T(8,128)(2,1)} %all-to-all-done.refs_0_, bf16[1,8,64,128]{3,2,1,0:T(8,128)(2,1)S(1)} %copy-done, ...), custom_call_target="tpu_custom_call" | custom-call | flops 1000 | bytes 100000000 | tf_op jit(solution)/shard_map/pallas_call | solution.py:272
  120.1 0.2 collective-permute-start.15
  120.4 1.3 collective-permute-start.16
  121.7 0.0 collective-permute-done.18.refs_5_
  121.7 0.4 collective-permute-start.17
  122.1 0.6 pad_maximum_fusion
  122.7 0.0 collective-permute-done.19.refs_6_
  122.7 0.0 collective-permute-done.20.refs_7_
  122.7 6.1 %collective-permute-done.15.refs_2_ = bf16[8,64,256]{2,1,0:T(8,128)(2,1)S(1)} collective-permute-done((bf16[8,64,256]{2,1,0:T(8,128)(2,1)S(1)}, bf16[8,64,256]{2,1,0:T(8,128)(2,1)S(1)}, u32[]{:S(2)}, u32[]{:S(2)}) %collective-permute-start.15) | collective-permute-done | bytes 262176 | tf_op jit(solution)/shard_map/ppermute | solution.py:314
  128.8 5.7 %collective-permute-done.16.refs_3_ = bf16[8,64,256]{2,1,0:T(8,128)(2,1)S(1)} collective-permute-done((bf16[8,64,256]{2,1,0:T(8,128)(2,1)S(1)}, bf16[8,64,256]{2,1,0:T(8,128)(2,1)S(1)}, u32[]{:S(2)}, u32[]{:S(2)}) %collective-permute-start.16) | collective-permute-done | bytes 262176 | tf_op jit(solution)/shard_map/ppermute | solution.py:314
  134.4 0.0 collective-permute-done.17.refs_4_
  134.4 1.5 %shard_map.54 = f32[64,16,256]{2,1,0:T(8,128)} custom-call(f32[8,64,256]{2,1,0:T(8,128)S(1)} %get-tuple-element.44.refs_0_, f32[8,64,256]{2,1,0:T(8,128)S(1)} %get-tuple-element.53.refs_1_, bf16[8,64,256]{2,1,0:T(8,128)(2,1)S(1)} %collective-permute-done.15.refs_2_, bf16[8,64,256]{2,1,0:T(8,128)(2,1)S(1)} %collective-permute-done.16.refs_3_, ...), custom_call_target="tpu_custom_call" | custom-call | flops 1000 | bytes 1000 | tf_op jit(solution)/shard_map/pallas_call | solution.py:302
  (2 shorter events, 0.0 us)
Async XLA Ops:
  10.6 7.4 %copy-start.3 = (f32[4,3,4,8,128]{4,3,2,1,0:T(8,128)S(1)}, f32[4,3,4,8,128]{4,3,2,1,0:T(8,128)}, u32[]{:S(2)}) copy-start(f32[4,3,4,8,128]{4,3,2,1,0:T(8,128)} %get-tuple-element.33) | copy-start | bytes 589828
  10.6 83.5 %all-to-all-start = ((bf16[8,16,64,128]{3,2,1,0:T(8,128)(2,1)}), bf16[8,16,64,128]{3,2,1,0:T(8,128)(2,1)}, u32[]{:S(2)}, u32[]{:S(2)}) async-start(bf16[8,16,64,128]{3,2,1,0:T(8,128)(2,1)} %get-tuple-element.32), calls=%async_computation | async-start | bytes 4194304 | tf_op jit(solution)/shard_map/all_to_all | solution.py:349
  18.0 2.5 %collective-permute-start = (f32[4,3,4,8,128]{4,3,2,1,0:T(8,128)S(1)}, f32[4,3,4,8,128]{4,3,2,1,0:T(8,128)S(1)}, u32[]{:S(2)}, u32[]{:S(2)}) collective-permute-start(f32[4,3,4,8,128]{4,3,2,1,0:T(8,128)S(1)} %copy-done.3), channel_id=1, source_target_pairs={{0,8},{8,16},{16,24},{1,9},{9,17},{17,25},{2,10},{10,18},{18,26},{... | collective-permute-start | bytes 589832 | tf_op jit(solution)/shard_map/ppermute | solution.py:351
  20.6 0.7 copy-start.2
  32.2 82.9 %copy-start = (bf16[1,8,64,128]{3,2,1,0:T(8,128)(2,1)S(1)}, bf16[1,8,64,128]{3,2,1,0:T(8,128)(2,1)}, u32[]{:S(2)}) copy-start(bf16[1,8,64,128]{3,2,1,0:T(8,128)(2,1)} %get-tuple-element.36.refs_1_) | copy-start | bytes 393220
  32.2 49.5 %collective-permute-start.8 = (bf16[1,8,64,128]{3,2,1,0:T(8,128)(2,1)}, bf16[1,8,64,128]{3,2,1,0:T(8,128)(2,1)S(1)}, u32[]{:S(2)}, u32[]{:S(2)}) collective-permute-start(bf16[1,8,64,128]{3,2,1,0:T(8,128)(2,1)} %get-tuple-element.46), channel_id=1, source_target_pairs={{0,4},{1,5},{2,6},{3,7},{4,0},{5,1},{6,2},{7,3},{8,12},{9,13},{10,... | collective-permute-start | bytes 393224 | tf_op jit(solution)/shard_map/ppermute | solution.py:314
  35.0 50.1 %collective-permute-start.9 = (bf16[1,8,64,128]{3,2,1,0:T(8,128)(2,1)}, bf16[1,8,64,128]{3,2,1,0:T(8,128)(2,1)S(1)}, u32[]{:S(2)}, u32[]{:S(2)}) collective-permute-start(bf16[1,8,64,128]{3,2,1,0:T(8,128)(2,1)} %get-tuple-element.47), channel_id=1, source_target_pairs={{0,5},{1,4},{2,7},{3,6},{4,1},{5,0},{6,3},{7,2},{8,13},{9,12},{10,... | collective-permute-start | bytes 393224 | tf_op jit(solution)/shard_map/ppermute | solution.py:314
  36.5 48.6 %collective-permute-start.10 = (bf16[1,8,64,128]{3,2,1,0:T(8,128)(2,1)}, bf16[1,8,64,128]{3,2,1,0:T(8,128)(2,1)S(1)}, u32[]{:S(2)}, u32[]{:S(2)}) collective-permute-start(bf16[1,8,64,128]{3,2,1,0:T(8,128)(2,1)} %get-tuple-element.48), channel_id=1, source_target_pairs={{0,6},{1,7},{2,4},{3,5},{4,2},{5,3},{6,0},{7,1},{8,14},{9,15},{10,... | collective-permute-start | bytes 393224 | tf_op jit(solution)/shard_map/ppermute | solution.py:314
  39.7 47.7 %collective-permute-start.11 = (bf16[1,8,64,128]{3,2,1,0:T(8,128)(2,1)}, bf16[1,8,64,128]{3,2,1,0:T(8,128)(2,1)S(1)}, u32[]{:S(2)}, u32[]{:S(2)}) collective-permute-start(bf16[1,8,64,128]{3,2,1,0:T(8,128)(2,1)} %get-tuple-element.49), channel_id=1, source_target_pairs={{0,7},{1,6},{2,5},{3,4},{4,3},{5,2},{6,1},{7,0},{8,15},{9,14},{10,... | collective-permute-start | bytes 393224 | tf_op jit(solution)/shard_map/ppermute | solution.py:314
  39.9 53.7 %collective-permute-start.12 = (bf16[1,8,64,128]{3,2,1,0:T(8,128)(2,1)}, bf16[1,8,64,128]{3,2,1,0:T(8,128)(2,1)S(1)}, u32[]{:S(2)}, u32[]{:S(2)}) collective-permute-start(bf16[1,8,64,128]{3,2,1,0:T(8,128)(2,1)} %get-tuple-element.50), channel_id=1, source_target_pairs={{0,1},{1,0},{2,3},{3,2},{4,5},{5,4},{6,7},{7,6},{8,9},{9,8},{10,11... | collective-permute-start | bytes 393224 | tf_op jit(solution)/shard_map/ppermute | solution.py:314
  81.7 12.4 %collective-permute-start.13 = (bf16[1,8,64,128]{3,2,1,0:T(8,128)(2,1)}, bf16[1,8,64,128]{3,2,1,0:T(8,128)(2,1)S(1)}, u32[]{:S(2)}, u32[]{:S(2)}) collective-permute-start(bf16[1,8,64,128]{3,2,1,0:T(8,128)(2,1)} %get-tuple-element.51), channel_id=1, source_target_pairs={{0,2},{1,3},{2,0},{3,1},{4,6},{5,7},{6,4},{7,5},{8,10},{9,11},{10,... | collective-permute-start | bytes 393224 | tf_op jit(solution)/shard_map/ppermute | solution.py:314
  85.1 9.0 %collective-permute-start.14 = (bf16[1,8,64,128]{3,2,1,0:T(8,128)(2,1)}, bf16[1,8,64,128]{3,2,1,0:T(8,128)(2,1)S(1)}, u32[]{:S(2)}, u32[]{:S(2)}) collective-permute-start(bf16[1,8,64,128]{3,2,1,0:T(8,128)(2,1)} %get-tuple-element.52), channel_id=1, source_target_pairs={{0,3},{1,2},{2,1},{3,0},{4,7},{5,6},{6,5},{7,4},{8,11},{9,10},{10,... | collective-permute-start | bytes 393224 | tf_op jit(solution)/shard_map/ppermute | solution.py:314
  85.1 18.4 %collective-permute-start.1 = (bf16[1,8,64,128]{3,2,1,0:T(8,128)(2,1)}, bf16[1,8,64,128]{3,2,1,0:T(8,128)(2,1)S(1)}, u32[]{:S(2)}, u32[]{:S(2)}) collective-permute-start(bf16[1,8,64,128]{3,2,1,0:T(8,128)(2,1)} %get-tuple-element.37), channel_id=1, source_target_pairs={{0,4},{1,5},{2,6},{3,7},{4,0},{5,1},{6,2},{7,3},{8,12},{9,13},{10,... | collective-permute-start | bytes 393224 | tf_op jit(solution)/shard_map/ppermute | solution.py:314
  87.4 17.9 %collective-permute-start.2 = (bf16[1,8,64,128]{3,2,1,0:T(8,128)(2,1)}, bf16[1,8,64,128]{3,2,1,0:T(8,128)(2,1)S(1)}, u32[]{:S(2)}, u32[]{:S(2)}) collective-permute-start(bf16[1,8,64,128]{3,2,1,0:T(8,128)(2,1)} %get-tuple-element.38), channel_id=1, source_target_pairs={{0,5},{1,4},{2,7},{3,6},{4,1},{5,0},{6,3},{7,2},{8,13},{9,12},{10,... | collective-permute-start | bytes 393224 | tf_op jit(solution)/shard_map/ppermute | solution.py:314
  93.7 11.7 %collective-permute-start.3 = (bf16[1,8,64,128]{3,2,1,0:T(8,128)(2,1)}, bf16[1,8,64,128]{3,2,1,0:T(8,128)(2,1)S(1)}, u32[]{:S(2)}, u32[]{:S(2)}) collective-permute-start(bf16[1,8,64,128]{3,2,1,0:T(8,128)(2,1)} %get-tuple-element.39), channel_id=1, source_target_pairs={{0,6},{1,7},{2,4},{3,5},{4,2},{5,3},{6,0},{7,1},{8,14},{9,15},{10,... | collective-permute-start | bytes 393224 | tf_op jit(solution)/shard_map/ppermute | solution.py:314
  94.1 0.9 copy-start.1
  95.0 5.3 %copy-start.7 = (bf16[1,8,64,128]{3,2,1,0:T(8,128)(2,1)S(1)}, bf16[1,8,64,128]{3,2,1,0:T(8,128)(2,1)}, u32[]{:S(2)}) copy-start(bf16[1,8,64,128]{3,2,1,0:T(8,128)(2,1)} %get-tuple-element.40) | copy-start | bytes 393220
  95.0 8.5 %copy-start.6 = (bf16[1,8,64,128]{3,2,1,0:T(8,128)(2,1)S(1)}, bf16[1,8,64,128]{3,2,1,0:T(8,128)(2,1)}, u32[]{:S(2)}) copy-start(bf16[1,8,64,128]{3,2,1,0:T(8,128)(2,1)} %get-tuple-element.41) | copy-start | bytes 393220
  95.0 10.3 %copy-start.5 = (bf16[1,8,64,128]{3,2,1,0:T(8,128)(2,1)S(1)}, bf16[1,8,64,128]{3,2,1,0:T(8,128)(2,1)}, u32[]{:S(2)}) copy-start(bf16[1,8,64,128]{3,2,1,0:T(8,128)(2,1)} %get-tuple-element.42) | copy-start | bytes 393220
  95.0 10.3 %copy-start.4 = (bf16[1,8,64,128]{3,2,1,0:T(8,128)(2,1)S(1)}, bf16[1,8,64,128]{3,2,1,0:T(8,128)(2,1)}, u32[]{:S(2)}) copy-start(bf16[1,8,64,128]{3,2,1,0:T(8,128)(2,1)} %get-tuple-element.43) | copy-start | bytes 393220
  100.1 21.6 %collective-permute-start.18 = (bf16[8,64,256]{2,1,0:T(8,128)(2,1)S(1)}, bf16[8,64,256]{2,1,0:T(8,128)(2,1)S(1)}, u32[]{:S(2)}, u32[]{:S(2)}) collective-permute-start(bf16[8,64,256]{2,1,0:T(8,128)(2,1)S(1)} %get-tuple-element.57), channel_id=1, source_target_pairs={{0,24},{8,16},{16,8},{24,0},{1,25},{9,17},{17,9},{25,1},{2,26},{10... | collective-permute-start | bytes 786440 | tf_op jit(solution)/shard_map/ppermute | solution.py:314
  100.3 10.6 %collective-permute-start.4 = (bf16[1,8,64,128]{3,2,1,0:T(8,128)(2,1)S(1)}, bf16[1,8,64,128]{3,2,1,0:T(8,128)(2,1)S(1)}, u32[]{:S(2)}, u32[]{:S(2)}) collective-permute-start(bf16[1,8,64,128]{3,2,1,0:T(8,128)(2,1)S(1)} %copy-done.7), channel_id=1, source_target_pairs={{0,7},{1,6},{2,5},{3,4},{4,3},{5,2},{6,1},{7,0},{8,15},{9,14},{10,... | collective-permute-start | bytes 393224 | tf_op jit(solution)/shard_map/ppermute | solution.py:314
  103.5 8.9 %collective-permute-start.5 = (bf16[1,8,64,128]{3,2,1,0:T(8,128)(2,1)S(1)}, bf16[1,8,64,128]{3,2,1,0:T(8,128)(2,1)S(1)}, u32[]{:S(2)}, u32[]{:S(2)}) collective-permute-start(bf16[1,8,64,128]{3,2,1,0:T(8,128)(2,1)S(1)} %copy-done.6), channel_id=1, source_target_pairs={{0,1},{1,0},{2,3},{3,2},{4,5},{5,4},{6,7},{7,6},{8,9},{9,8},{10,11... | collective-permute-start | bytes 393224 | tf_op jit(solution)/shard_map/ppermute | solution.py:314
  105.3 7.2 %collective-permute-start.6 = (bf16[1,8,64,128]{3,2,1,0:T(8,128)(2,1)S(1)}, bf16[1,8,64,128]{3,2,1,0:T(8,128)(2,1)S(1)}, u32[]{:S(2)}, u32[]{:S(2)}) collective-permute-start(bf16[1,8,64,128]{3,2,1,0:T(8,128)(2,1)S(1)} %copy-done.5), channel_id=1, source_target_pairs={{0,2},{1,3},{2,0},{3,1},{4,6},{5,7},{6,4},{7,5},{8,10},{9,11},{10,... | collective-permute-start | bytes 393224 | tf_op jit(solution)/shard_map/ppermute | solution.py:314
  105.3 9.7 %collective-permute-start.7 = (bf16[1,8,64,128]{3,2,1,0:T(8,128)(2,1)S(1)}, bf16[1,8,64,128]{3,2,1,0:T(8,128)(2,1)S(1)}, u32[]{:S(2)}, u32[]{:S(2)}) collective-permute-start(bf16[1,8,64,128]{3,2,1,0:T(8,128)(2,1)S(1)} %copy-done.4), channel_id=1, source_target_pairs={{0,3},{1,2},{2,1},{3,0},{4,7},{5,6},{6,5},{7,4},{8,11},{9,10},{10,... | collective-permute-start | bytes 393224 | tf_op jit(solution)/shard_map/ppermute | solution.py:314
  110.9 11.7 %collective-permute-start.19 = (bf16[8,64,256]{2,1,0:T(8,128)(2,1)S(1)}, bf16[8,64,256]{2,1,0:T(8,128)(2,1)S(1)}, u32[]{:S(2)}, u32[]{:S(2)}) collective-permute-start(bf16[8,64,256]{2,1,0:T(8,128)(2,1)S(1)} %get-tuple-element.58), channel_id=1, source_target_pairs={{0,16},{8,24},{16,0},{24,8},{1,17},{9,25},{17,1},{25,9},{2,18},{10... | collective-permute-start | bytes 786440 | tf_op jit(solution)/shard_map/ppermute | solution.py:314
  112.4 10.3 %collective-permute-start.20 = (bf16[8,64,256]{2,1,0:T(8,128)(2,1)S(1)}, bf16[8,64,256]{2,1,0:T(8,128)(2,1)S(1)}, u32[]{:S(2)}, u32[]{:S(2)}) collective-permute-start(bf16[8,64,256]{2,1,0:T(8,128)(2,1)S(1)} %get-tuple-element.59), channel_id=1, source_target_pairs={{0,8},{8,0},{16,24},{24,16},{1,9},{9,1},{17,25},{25,17},{2,10},{10... | collective-permute-start | bytes 786440 | tf_op jit(solution)/shard_map/ppermute | solution.py:314
  120.1 8.6 %collective-permute-start.15 = (bf16[8,64,256]{2,1,0:T(8,128)(2,1)S(1)}, bf16[8,64,256]{2,1,0:T(8,128)(2,1)S(1)}, u32[]{:S(2)}, u32[]{:S(2)}) collective-permute-start(bf16[8,64,256]{2,1,0:T(8,128)(2,1)S(1)} %get-tuple-element.54), channel_id=1, source_target_pairs={{0,24},{8,16},{16,8},{24,0},{1,25},{9,17},{17,9},{25,1},{2,26},{10... | collective-permute-start | bytes 786440 | tf_op jit(solution)/shard_map/ppermute | solution.py:314
  120.4 14.1 %collective-permute-start.16 = (bf16[8,64,256]{2,1,0:T(8,128)(2,1)S(1)}, bf16[8,64,256]{2,1,0:T(8,128)(2,1)S(1)}, u32[]{:S(2)}, u32[]{:S(2)}) collective-permute-start(bf16[8,64,256]{2,1,0:T(8,128)(2,1)S(1)} %get-tuple-element.55), channel_id=1, source_target_pairs={{0,16},{8,24},{16,0},{24,8},{1,17},{9,25},{17,1},{25,9},{2,18},{10... | collective-permute-start | bytes 786440 | tf_op jit(solution)/shard_map/ppermute | solution.py:314
  121.7 12.7 %collective-permute-start.17 = (bf16[8,64,256]{2,1,0:T(8,128)(2,1)S(1)}, bf16[8,64,256]{2,1,0:T(8,128)(2,1)S(1)}, u32[]{:S(2)}, u32[]{:S(2)}) collective-permute-start(bf16[8,64,256]{2,1,0:T(8,128)(2,1)S(1)} %get-tuple-element.56), channel_id=1, source_target_pairs={{0,8},{8,0},{16,24},{24,16},{1,9},{9,1},{17,25},{25,17},{2,10},{10... | collective-permute-start | bytes 786440 | tf_op jit(solution)/shard_map/ppermute | solution.py:314
